TPU v7x, 512 devices: a whole 4x8x8 slice. The times are simulated.
512 devices in a mesh: island: 32 (over y, x), member: 16 (over z, core).
Axes of the slice: x: 4, y: 8, z: 8, core: 2. Of those that a mesh axis runs over, the one named last changes fastest.
Arguments:
- tokens: bfloat16 [32, 2304, 5120], P('island', 'member'), may hold values from -6 to 6
- cotangent: bfloat16 [32, 2048, 768], P('island', 'member'), may hold values from -6 to 6
- slot_token: int32 [32, 2048], P('island', 'member'), may hold values from 0 to 143, as said below
- outer_weight: float32 [5120, 768], P('member', 'island'), may hold values from -5 to 5
- outer_momentum: float32 [5120, 768], P('member', 'island'), may hold values from -2 to 2
- first_moment: float32 [32, 5120, 768], P('island', 'member'), may hold values from -0.4 to 0.4
- second_moment: float32 [32, 5120, 768], P('island', 'member'), may hold values from 0.002 to 0.02
- error_state: bfloat16 [32, 5120, 768], P('island', 'member'), may hold values from -0.3984375 to 0.3984375
Outputs:
- new_outer: float32 [5120, 768], P('member', 'island')
- new_momentum: float32 [5120, 768], P('member', 'island')
Inputs may be any that keep to these rules, and one draw needn't show every extreme that they name: `slot_token`: within the 128 slots filled by one member of one replica, the indices are distinct.
All inputs are finite; a program needn't handle non-finite values.
Results may differ from a plain program's by a relative error of at most 0.003.
Values may be sent and summed in bfloat16 or wider, within the bound.
No kernel may reach another device: no remote copies, remote signals or barrier semaphores. Data moves between devices by JAX's collectives and lax.ppermute only.
A program may use at most 64 MiB of HBM per device.

v0:
```python
import jax
import jax.numpy as jnp
from jax import lax
from jax.sharding import PartitionSpec as P


def silu_grad(values):
    sigmoid = jax.nn.sigmoid(values)
    return sigmoid * (1.0 + values * (1.0 - sigmoid))


def local(
    tokens,
    cotangent,
    slot_token,
    outer_weight,
    outer_momentum,
    first_moment,
    second_moment,
    error_state,
):
    fan_scale = float(tokens.shape[2]) ** (-0.5)
    weight = lax.all_gather(outer_weight, "island", axis=1, tiled=True)
    weight_low = weight.astype(jnp.bfloat16)
    picked = jnp.take(tokens[0], slot_token[0], axis=0)
    routed = lax.all_to_all(picked, "member", split_axis=1, concat_axis=0, tiled=True)
    row_block = routed
    pre_act = lax.psum_scatter(
        (jnp.dot(row_block, weight_low, preferred_element_type=jnp.float32) * fan_scale).astype(
            jnp.bfloat16
        ),
        "member",
        scatter_dimension=0,
        tiled=True,
    ).astype(jnp.float32)
    hidden_grad = (cotangent[0].astype(jnp.float32) * silu_grad(pre_act)).astype(jnp.bfloat16)
    row_block = routed
    contracted = lax.dot_general(
        row_block,
        lax.all_gather(hidden_grad, "member", axis=0, tiled=True),
        (((0,), (0,)), ((), ())),
        preferred_element_type=jnp.float32,
    )
    inner_grad = contracted * fan_scale
    moment_one = 0.9 * first_moment[0] + 0.1 * inner_grad
    moment_two = 0.95 * second_moment[0] + 0.05 * inner_grad * inner_grad
    pseudo_grad = 0.25 * (moment_one / (jnp.sqrt(moment_two) + 1e-08) + 0.1 * weight)
    compressed = (pseudo_grad + error_state[0].astype(jnp.float32)).astype(jnp.bfloat16)
    summed = lax.psum_scatter(
        compressed.astype(jnp.float32).astype(jnp.bfloat16),
        "island",
        scatter_dimension=1,
        tiled=True,
    ).astype(jnp.float32)
    averaged = summed / float(lax.axis_size("island"))
    new_momentum = 0.9 * outer_momentum + averaged
    new_outer = outer_weight - 0.7 * (averaged + 0.9 * new_momentum)
    return (new_outer, new_momentum)


def solution(mesh):
    in_specs = (
        P("island", "member", None),
        P("island", "member", None),
        P("island", "member"),
        P("member", "island"),
        P("member", "island"),
        P("island", "member", None),
        P("island", "member", None),
        P("island", "member", None),
    )
    out_specs = (P("member", "island"), P("member", "island"))
    return jax.shard_map(local, mesh=mesh, in_specs=in_specs, out_specs=out_specs, check_vma=False)
```

profile of v0, /device:TPU:16, one launch (start us, length us, event | category | flops | bytes accessed | tf_op | source)
XLA Modules:
  0.0 357.6 jit_solution(14162507811344015966)
XLA Ops:
  7.2 0.0 copy-start
  7.2 0.8 fusion.21
  8.0 0.7 compare_and_fusion
  8.6 0.0 copy-done
  8.6 1.3 gather_fusion
  9.9 1.4 copy.29
  11.4 2.5 broadcast_select_fusion
  13.9 0.0 copy-start.2
  13.9 10.6 %all-to-all-start = ((bf16[128,16,320]{0,2,1:T(8,128)(2,1)}), bf16[128,16,320]{0,2,1:T(8,128)(2,1)}, u32[]{:S(2)}, u32[]{:S(2)}) async-start(bf16[128,16,320]{0,2,1:T(8,128)(2,1)} %broadcast_select_fusion), calls=%async_computation | async-start | bytes 2621440 | tf_op jit(solution)/shard_map/all_to_all | solution.py:26
  24.5 0.0 reduce-scatter.3.cloned.1.call-start
  24.6 0.0 copy-done.2
  24.6 50.7 %all_gather.6 = f32[320,768]{0,1:T(8,128)S(1)} all-gather(f32[320,24]{0,1:T(8,128)S(1)} %copy-done.2), channel_id=1, replica_groups=mesh['island'=32,'member'=16] {'island'}, dimensions={1}, use_global_device_ids=true | all-gather | bytes 1013760 | tf_op jit(solution)/shard_map/all_gather | solution.py:23
  75.3 0.0 all-to-all-done
  75.3 4.8 %multiply_convert_fusion = bf16[2048,768]{1,0:T(8,128)(2,1)} fusion(f32[320,768]{0,1:T(8,128)S(1)} %all_gather.6, bf16[128,16,320]{0,2,1:T(8,128)(2,1)} %all-to-all-done), kind=kOutput, calls=%fused_computation.1 | convolution fusion | flops 1010024448 | bytes 5439488 | tf_op jit(solution)/shard_map/dot_general | solution.py:29
  80.1 0.0 copy-start.1
  80.1 0.0 reduce-scatter.3.cloned.1.call-update
  80.1 0.0 all-gather.2.cloned.1.call-start
  80.1 63.1 %reduce-scatter.3.cloned.1.call-done = bf16[128,768]{1,0:T(8,128)(2,1)} async-done(((bf16[2048,768]{1,0:T(8,128)(2,1)}), bf16[128,768]{1,0:T(8,128)(2,1)}) %reduce-scatter.3.cloned.1.call-update) | async-done | bytes 196624 | tf_op jit(solution)/shard_map/reduce_scatter | solution.py:28
  143.2 0.0 copy-done.1
  143.2 1.8 fusion.20
  145.0 0.0 copy-start.4
  145.0 0.0 all-gather.2.cloned.1.call-update
  145.0 0.0 all-reduce.3.cloned.1.call-start
  145.1 1.3 copy.31
  146.4 0.0 copy-start.3
  146.4 41.3 %all-gather.2.cloned.1.call-done = bf16[2048,768]{1,0:T(8,128)(2,1)} async-done(((bf16[128,768]{1,0:T(8,128)(2,1)}), bf16[2048,768]{1,0:T(8,128)(2,1)}) %all-gather.2.cloned.1.call-update) | async-done | bytes 3145744 | tf_op jit(solution)/shard_map/all_gather | solution.py:40
  187.7 0.0 copy-done.4
  187.7 5.7 %fusion.5 = bf16[320,768]{1,0:T(8,128)(2,1)} fusion(f32[320,768]{1,0:T(8,128)} %copy.31, f32[1,320,768]{2,1,0:T(8,128)} %param.14, f32[1,320,768]{2,1,0:T(8,128)} %param.13, bf16[2048,768]{1,0:T(8,128)(2,1)} %all-gather.2.cloned.1.call-done, bf16[1,320,768]{2,1,0:T(8,128)(2,1)S(1)} %copy-done.4, bf16[128,16,320]{0,2,1:T(8,128)(2,1)} %all-to-all-done), kind=kOutput, calls=%fused_computation.9 | convolution fusion | flops 1010565120 | bytes 8388608 | tf_op jit(solution)/shard_map/dot_general | solution.py:38
  193.4 0.0 all-reduce.3.cloned.1.call-update
  193.4 1.3 dynamic-slice
  195.3 154.0 %all-reduce.3.cloned.1.call-done = bf16[320,768]{1,0:T(8,128)(2,1)} async-done(((bf16[320,768]{1,0:T(8,128)(2,1)}), bf16[320,768]{1,0:T(8,128)(2,1)}) %all-reduce.3.cloned.1.call-update) | async-done | bytes 491536
  349.3 1.0 constant_dynamic-slice_fusion
  350.3 0.1 copy.32
  350.4 0.0 copy-done.3
  350.4 0.6 multiply_subtract_fusion
  (1 shorter events, 0.0 us)
Async XLA Ops:
  7.2 1.5 copy-start
  13.9 10.7 %copy-start.2 = (f32[320,24]{0,1:T(8,128)S(1)}, f32[320,24]{0,1:T(8,128)}, u32[]{:S(2)}) copy-start(f32[320,24]{0,1:T(8,128)} %param.11) | copy-start | bytes 92164
  13.9 61.3 %all-to-all-start = ((bf16[128,16,320]{0,2,1:T(8,128)(2,1)}), bf16[128,16,320]{0,2,1:T(8,128)(2,1)}, u32[]{:S(2)}, u32[]{:S(2)}) async-start(bf16[128,16,320]{0,2,1:T(8,128)(2,1)} %broadcast_select_fusion), calls=%async_computation | async-start | bytes 2621440 | tf_op jit(solution)/shard_map/all_to_all | solution.py:26
  24.5 118.7 %reduce-scatter.3.cloned.1.call-start = ((), (), s32[]{:S(2)}) async-start(), calls=%async_computation.2 | async-start | bytes 3342336 | tf_op jit(solution)/shard_map/reduce_scatter | solution.py:28
  80.1 63.2 %copy-start.1 = (bf16[1,128,768]{2,1,0:T(8,128)(2,1)S(1)}, bf16[1,128,768]{2,1,0:T(8,128)(2,1)}, u32[]{:S(2)}) copy-start(bf16[1,128,768]{2,1,0:T(8,128)(2,1)} %param.9) | copy-start | bytes 589828
  80.1 107.6 %all-gather.2.cloned.1.call-start = ((), (), s32[]{:S(2)}) async-start(), calls=%async_computation.3 | async-start | bytes 3342336 | tf_op jit(solution)/shard_map/all_gather | solution.py:40
  145.0 42.7 %copy-start.4 = (bf16[1,320,768]{2,1,0:T(8,128)(2,1)S(1)}, bf16[1,320,768]{2,1,0:T(8,128)(2,1)}, u32[]{:S(2)}) copy-start(bf16[1,320,768]{2,1,0:T(8,128)(2,1)} %param.15) | copy-start | bytes 1474564
  145.0 204.3 %all-reduce.3.cloned.1.call-start = ((), (), s32[]{:S(2)}) async-start(), calls=%async_computation.4 | async-start | bytes 983040
  146.4 204.0 %copy-start.3 = (f32[320,24]{0,1:T(8,128)S(1)}, f32[320,24]{0,1:T(8,128)}, u32[]{:S(2)}) copy-start(f32[320,24]{0,1:T(8,128)} %param.12) | copy-start | bytes 92164
Sparse Core Ops, SparseCore 0:
  80.2 62.9 reduce-scatter.2
  145.3 42.3 all-gather.1
  193.5 155.7 all-reduce.2
where the time goes:
time: 358 us
  waiting for transfers between devices  258 us (72%)
  blocking collectives  50.7 us (14%)
  between operations  14.5 us (4%)
  starting transfers between devices  10.7 us (3%)
  matrix products  10.5 us (3%)
  local copies, waits for them, and re-layouts  6.46 us (2%)
  other arithmetic  6.4 us (2%)
    unnamed x4, waiting for transfers between devices  154 us
    reduce_scatter x1, waiting for transfers between devices, local(): lax.psum_scatter((jnp.dot(row_block, weight_low, preferred_element_type=j...  63.1 us
    all_gather x1, blocking collectives, local(): weight = lax.all_gather(outer_weight, 'island', axis=1, tiled=True)  50.7 us
    all_gather x1, waiting for transfers between devices, local(): lax.all_gather(hidden_grad, 'member', axis=0, tiled=True)  41.3 us
    all_to_all x1, starting transfers between devices, local(): lax.all_to_all(picked, 'member', split_axis=1, concat_axis=0, tiled=True)  10.6 us
  transfers between devices with their start and end apart: 4, of which 3 were waited for; matrix products, arithmetic and copies ran while one was open for 1% of the time, Pallas kernels for 0%

commit v1 on v0

v1 whole, which is shorter than its diff:
```python
import jax
import jax.numpy as jnp
from jax import lax
from jax.experimental import pallas as pl
from jax.experimental.pallas import tpu as pltpu
from jax.sharding import PartitionSpec as P

NY, NX, NM = 8, 4, 16
ALONG_X = [[y * NX + x for x in range(NX)] for y in range(NY)]
ALONG_Y = [[y * NX + x for y in range(NY)] for x in range(NX)]
BF = jnp.bfloat16
F32 = jnp.float32


def spread(block, groups):
    n = len(groups[0])
    return lax.all_to_all(
        jnp.broadcast_to(block[None], (n,) + block.shape),
        "island",
        split_axis=0,
        concat_axis=0,
        tiled=True,
        axis_index_groups=groups,
    )


def hidden_kernel(scale, x_ref, w_ref, cot_ref, out_ref, acc_ref):
    step = pl.program_id(0)
    total = None
    for m in range(x_ref.shape[0]):
        part = lax.dot_general(
            x_ref[m], w_ref[m], (((0,), (0,)), ((), ())), preferred_element_type=F32
        )
        total = part if total is None else total + part

    @pl.when(step == 0)
    def _():
        acc_ref[...] = total

    @pl.when(step > 0)
    def _():
        acc_ref[...] += total

    @pl.when(step == pl.num_programs(0) - 1)
    def _():
        pre = acc_ref[...] * scale
        sig = 1.0 / (1.0 + jnp.exp(-pre))
        grad = sig * (1.0 + pre * (1.0 - sig))
        out_ref[...] = (cot_ref[...].astype(F32) * grad).astype(BF)


def hidden(xt, w, cot, scale):
    nm, rows, slots = xt.shape
    ff = w.shape[2]
    per = 2
    return pl.pallas_call(
        lambda *refs: hidden_kernel(scale, *refs),
        grid=(nm // per,),
        in_specs=[
            pl.BlockSpec((per, rows, slots), lambda i: (i, 0, 0)),
            pl.BlockSpec((per, rows, ff), lambda i: (i, 0, 0)),
            pl.BlockSpec((slots, ff), lambda i: (0, 0)),
        ],
        out_specs=pl.BlockSpec((slots, ff), lambda i: (0, 0)),
        out_shape=jax.ShapeDtypeStruct((slots, ff), BF),
        scratch_shapes=[pltpu.VMEM((slots, ff), F32)],
        compiler_params=pltpu.CompilerParams(vmem_limit_bytes=24 * 2**20),
        cost_estimate=pl.CostEstimate(
            flops=2 * nm * rows * slots * ff,
            bytes_accessed=2 * (xt.size + w.size + 2 * cot.size),
            transcendentals=cot.size,
        ),
        name="hidden",
    )(xt, w, cot)


def step_kernel(scale, x_ref, h_ref, m1_ref, m2_ref, err_ref, out_ref):
    total = None
    for m in range(0, x_ref.shape[0], 2):
        left = jnp.concatenate([x_ref[m], x_ref[m + 1]], axis=1)
        right = jnp.concatenate([h_ref[m], h_ref[m + 1]], axis=0)
        part = jnp.dot(left, right, preferred_element_type=F32)
        total = part if total is None else total + part
    grad = total * scale
    one = 0.9 * m1_ref[...] + 0.1 * grad
    two = 0.95 * m2_ref[...] + 0.05 * grad * grad
    moved = 0.25 * (one / (jnp.sqrt(two) + 1e-08)) + err_ref[...].astype(F32)
    out_ref[...] = moved.T.astype(BF)


def inner_step(xt, h, m1, m2, err, scale):
    nm, rows, slots = xt.shape
    ff = h.shape[2]
    blk = 256
    return pl.pallas_call(
        lambda *refs: step_kernel(scale, *refs),
        grid=(ff // blk,),
        in_specs=[
            pl.BlockSpec((nm, rows, slots), lambda i: (0, 0, 0)),
            pl.BlockSpec((nm, slots, blk), lambda i: (0, 0, i)),
            pl.BlockSpec((rows, blk), lambda i: (0, i)),
            pl.BlockSpec((rows, blk), lambda i: (0, i)),
            pl.BlockSpec((rows, blk), lambda i: (0, i)),
        ],
        out_specs=pl.BlockSpec((blk, rows), lambda i: (i, 0)),
        out_shape=jax.ShapeDtypeStruct((ff, rows), BF),
        compiler_params=pltpu.CompilerParams(vmem_limit_bytes=24 * 2**20),
        cost_estimate=pl.CostEstimate(
            flops=2 * nm * rows * slots * ff,
            bytes_accessed=2 * (xt.size + h.size) + 12 * rows * ff,
            transcendentals=2 * rows * ff,
        ),
        name="inner_step",
    )(xt, h, m1, m2, err)


def local(
    tokens,
    cotangent,
    slot_token,
    outer_weight,
    outer_momentum,
    first_moment,
    second_moment,
    error_state,
):
    dim = tokens.shape[2]
    scale = float(dim) ** (-0.5)
    rows, cols = outer_weight.shape
    slots = slot_token.shape[1]
    weight_t = outer_weight.T

    low = weight_t.astype(BF)
    block = spread(low, ALONG_Y).reshape(NY * cols, rows)
    block = spread(block, ALONG_X).reshape(NX, NY, cols, rows)
    block = block.transpose(1, 0, 2, 3).reshape(NX * NY * cols, rows).T
    weights = lax.all_gather(block, "member", axis=0, tiled=False)

    chosen = lax.broadcasted_iota(jnp.int32, (tokens.shape[1], slots), 0) == slot_token
    picked = lax.dot_general(
        tokens[0],
        chosen.astype(BF),
        (((0,), (0,)), ((), ())),
        preferred_element_type=F32,
    ).astype(BF)
    picked = picked.reshape(NM, rows, slots)

    hid = hidden(picked, weights, cotangent[0], scale)
    picked, hid = lax.optimization_barrier((picked, hid))
    routed = lax.all_to_all(picked, "member", split_axis=0, concat_axis=0, tiled=True)
    hid_all = lax.all_gather(hid, "member", axis=0, tiled=False)
    moved = inner_step(
        routed, hid_all, first_moment[0], second_moment[0], error_state[0], scale
    )
    parts = lax.all_to_all(
        moved.reshape(NX * NY, cols, rows), "island", split_axis=0, concat_axis=0, tiled=True
    )
    averaged = jnp.sum(parts.astype(F32), axis=0) / float(NX * NY) + 0.025 * weight_t
    new_momentum = 0.9 * outer_momentum.T + averaged
    new_outer = weight_t - 0.7 * (averaged + 0.9 * new_momentum)
    return (new_outer.T, new_momentum.T)


def solution(mesh):
    in_specs = (
        P("island", "member", None),
        P("island", "member", None),
        P("island", "member"),
        P("member", "island"),
        P("member", "island"),
        P("island", "member", None),
        P("island", "member", None),
        P("island", "member", None),
    )
    out_specs = (P("member", "island"), P("member", "island"))
    return jax.shard_map(local, mesh=mesh, in_specs=in_specs, out_specs=out_specs, check_vma=False)
```

time: 358 us -> 203 us (0.57)
  the two profiles are of different devices: /device:TPU:16 before, /device:TPU:8 now
where the time goes in v1:
time: 203 us
  blocking collectives  104 us (51%)
  waiting for transfers between devices  62.4 us (31%)
  between operations  14.1 us (7%)
  local copies, waits for them, and re-layouts  11.8 us (6%)
  Pallas kernels  7.14 us (4%)
    all_gather x1, waiting for transfers between devices, local(): weights = lax.all_gather(block, 'member', axis=0, tiled=False)  52.5 us
    all_to_all x1, blocking collectives, local(): lax.all_to_all(picked, 'member', split_axis=0, concat_axis=0, tiled=True)  47.3 us
    all_to_all x1, blocking collectives, local(): lax.all_to_all(moved.reshape(NX * NY, cols, rows), 'island', split_axis=0...  28.6 us
    all_to_all x2, blocking collectives, spread(): lax.all_to_all(jnp.broadcast_to(block[None], (n,) + block.shape), 'island...  28.2 us
    all_gather x1, waiting for transfers between devices, local(): hid_all = lax.all_gather(hid, 'member', axis=0, tiled=False)  9.88 us
    unnamed x22, local copies, waits for them, and re-layouts  8.87 us
    pallas_call x1, Pallas kernels, hidden(): pl.pallas_call(lambda *refs: hidden_kernel(scale, *refs), grid=(nm // per...  4.42 us
  transfers between devices with their start and end apart: 2, of which 2 were waited for; matrix products, arithmetic and copies ran while one was open for 2% of the time, Pallas kernels for 0%

profile of v1, /device:TPU:8, one launch (start us, length us, event | category | flops | bytes accessed | tf_op | source)
XLA Modules:
  0.0 202.9 jit_solution(5208204973652679232)
XLA Ops:
  7.2 0.0 copy-start
  7.2 0.0 all-gather.5.cloned.1.call-start
  7.2 0.9 convert_bitcast_fusion
  8.1 16.0 %all_to_all.20 = bf16[8,24,320]{2,1,0:T(8,128)(2,1)S(1)} all-to-all(bf16[8,24,320]{2,1,0:T(8,128)(2,1)S(1)} %broadcast_in_dim.6), channel_id=1, replica_groups={{0,64,128,192,256,320,384,448},{16,80,144,208,272,336,400,464},{32,96,1..., dimensions={0} | all-to-all | bytes 245760 | tf_op jit(solution)/shard_map/all_to_all | solution.py:17
  24.1 0.1 broadcast_in_dim.15
  24.2 12.2 %all_to_all.21 = bf16[4,192,320]{2,1,0:T(8,128)(2,1)S(1)} all-to-all(bf16[4,192,320]{2,1,0:T(8,128)(2,1)S(1)} %broadcast_in_dim.15), channel_id=1, replica_groups={{0,16,32,48},{64,80,96,112},{128,144,160,176},{192,208,224,240},{256,27..., dimensions={0} | all-to-all | bytes 983040 | tf_op jit(solution)/shard_map/all_to_all | solution.py:17
  36.4 0.0 copy-start.10
  36.4 0.1 copy.15
  36.4 1.0 copy.16
  37.5 0.0 all-gather.5.cloned.1.call-update
  37.5 0.0 all-gather.7.cloned.1.call-start
  37.5 0.0 copy-done
  37.5 0.0 copy-done.10
  37.5 1.7 fusion
  39.3 0.0 copy-start.7
  39.3 1.8 copy.14
  41.1 52.5 %all-gather.5.cloned.1.call-done = bf16[5120,768]{1,0:T(8,128)(2,1)} async-done(((bf16[320,768]{1,0:T(8,128)(2,1)}), bf16[5120,768]{1,0:T(8,128)(2,1)}) %all-gather.5.cloned.1.call-update) | async-done | bytes 7864336 | tf_op jit(solution)/shard_map/all_gather | solution.py:137
  93.5 0.0 copy-done.7
  93.5 0.0 copy-start.1
  93.5 3.2 %copy-done.1 = bf16[5120,768]{1,0:T(8,128)(2,1)S(1)} copy-done((bf16[5120,768]{1,0:T(8,128)(2,1)S(1)}, bf16[5120,768]{1,0:T(8,128)(2,1)}, u32[]{:S(2)}) %copy-start.1) | copy-done | bytes 7864344
  96.8 4.4 %hidden.1 = bf16[128,768]{1,0:T(8,128)(2,1)} custom-call(bf16[16,320,128]{2,1,0:T(8,128)(2,1)S(1)} %bitcast.30, bf16[16,320,768]{2,1,0:T(8,128)(2,1)S(1)} %bitcast.32, bf16[128,768]{1,0:T(8,128)(2,1)S(1)} %bitcast.38), custom_call_target="tpu_custom_call" | custom-call | flops 1006632960 | bytes 9568256 | tf_op jit(solution)/shard_map/hidden/pallas_call | solution.py:56
  101.2 0.0 copy-start.6
  101.2 0.0 all-gather.7.cloned.1.call-update
  101.2 47.3 %all_to_all.22.refs_0_ = bf16[16,320,128]{2,1,0:T(8,128)(2,1)} all-to-all(bf16[16,320,128]{2,1,0:T(8,128)(2,1)S(1)} %bitcast.31), channel_id=1, replica_groups=mesh['island'=32,'member'=16] {'member'}, dimensions={0} | all-to-all | bytes 2621440 | tf_op jit(solution)/shard_map/all_to_all | solution.py:150
  148.5 9.9 %all-gather.7.cloned.1.call-done = bf16[2048,768]{1,0:T(8,128)(2,1)} async-done(((bf16[128,768]{1,0:T(8,128)(2,1)}), bf16[2048,768]{1,0:T(8,128)(2,1)}) %all-gather.7.cloned.1.call-update) | async-done | bytes 3145744 | tf_op jit(solution)/shard_map/all_gather | solution.py:151
  158.4 0.0 copy-done.6
  158.4 0.0 copy-start.2
  158.4 1.3 copy-done.2
  159.7 0.0 copy-start.3
  159.7 1.9 copy-done.3
  161.6 0.0 copy-start.4
  161.6 1.2 copy-done.4
  162.8 0.0 copy-start.5
  162.8 1.2 copy-done.5
  164.0 2.7 %inner_step.1 = bf16[768,320]{1,0:T(8,128)(2,1)S(1)} custom-call(bf16[16,320,128]{2,1,0:T(8,128)(2,1)S(1)} %copy-done.2, bf16[16,128,768]{2,1,0:T(8,128)(2,1)S(1)} %bitcast.33, f32[320,768]{1,0:T(8,128)S(1)} %bitcast.35, f32[320,768]{1,0:T(8,128)S(1)} %bitcast.36, bf16[320,768]{1,0:T(8,128)(2,1)S(1)} %bitcast.37), custom_call_target="tpu_custom_call" | custom-call | flops 1006632960 | bytes 7405568 | tf_op jit(solution)/shard_map/inner_step/pallas_call | solution.py:95
  166.7 0.0 copy-start.8
  166.7 0.0 copy-start.9
  166.7 28.6 %all_to_all.23 = bf16[32,24,320]{2,1,0:T(8,128)(2,1)S(1)} all-to-all(bf16[32,24,320]{2,1,0:T(8,128)(2,1)S(1)} %bitcast.34), channel_id=1, replica_groups=mesh['island'=32,'member'=16] {'island'}, dimensions={0} | all-to-all | bytes 983040 | tf_op jit(solution)/shard_map/all_to_all | solution.py:155
  195.3 0.1 convert_reduce_fusion
  195.4 0.0 copy-done.8
  195.4 0.0 copy-done.9
  195.5 0.6 multiply_subtract_fusion
  (1 shorter events, 0.0 us)
Async XLA Ops:
  7.2 30.4 %copy-start = (bf16[1,144,5120]{2,1,0:T(8,128)(2,1)S(1)}, bf16[1,144,5120]{2,1,0:T(8,128)(2,1)}, u32[]{:S(2)}) copy-start(bf16[1,144,5120]{2,1,0:T(8,128)(2,1)} %param.8) | copy-start | bytes 4423684
  7.2 86.3 %all-gather.5.cloned.1.call-start = ((), (), s32[]{:S(2)}) async-start(), calls=%async_computation.4 | async-start | bytes 8355840 | tf_op jit(solution)/shard_map/all_gather | solution.py:137
  36.4 1.2 copy-start.10
  37.5 120.9 %all-gather.7.cloned.1.call-start = ((), (), s32[]{:S(2)}) async-start(), calls=%async_computation.5 | async-start | bytes 3342336 | tf_op jit(solution)/shard_map/all_gather | solution.py:151
  39.3 54.3 %copy-start.7 = (bf16[1,128,768]{2,1,0:T(8,128)(2,1)S(1)}, bf16[1,128,768]{2,1,0:T(8,128)(2,1)}, u32[]{:S(2)}) copy-start(bf16[1,128,768]{2,1,0:T(8,128)(2,1)} %param.9) | copy-start | bytes 589828
  93.5 3.2 %copy-start.1 = (bf16[5120,768]{1,0:T(8,128)(2,1)S(1)}, bf16[5120,768]{1,0:T(8,128)(2,1)}, u32[]{:S(2)}) copy-start(bf16[5120,768]{1,0:T(8,128)(2,1)} %all-gather.5.cloned.1.call-done) | copy-start | bytes 23592964
  101.2 57.2 %copy-start.6 = (bf16[1,320,768]{2,1,0:T(8,128)(2,1)S(1)}, bf16[1,320,768]{2,1,0:T(8,128)(2,1)}, u32[]{:S(2)}) copy-start(bf16[1,320,768]{2,1,0:T(8,128)(2,1)} %param.15) | copy-start | bytes 1474564
  158.4 1.3 copy-start.2
  159.7 1.9 copy-start.3
  161.6 1.2 copy-start.4
  162.8 1.2 copy-start.5
  166.7 28.7 %copy-start.8 = (f32[320,24]{0,1:T(8,128)S(1)}, f32[320,24]{0,1:T(8,128)}, u32[]{:S(2)}) copy-start(f32[320,24]{0,1:T(8,128)} %param.11) | copy-start | bytes 92164
  166.7 28.7 %copy-start.9 = (f32[320,24]{0,1:T(8,128)S(1)}, f32[320,24]{0,1:T(8,128)}, u32[]{:S(2)}) copy-start(f32[320,24]{0,1:T(8,128)} %param.12) | copy-start | bytes 92164
Sparse Core Ops, SparseCore 0:
  37.6 55.8 all-gather.4
  101.3 56.9 all-gather.6

commit v2 on v0

v2 whole, which is shorter than its diff:
```python
import jax
import jax.numpy as jnp
from jax import lax
from jax.experimental import pallas as pl
from jax.experimental.pallas import tpu as pltpu
from jax.sharding import PartitionSpec as P

NY, NX, NA = 8, 4, 4
ALONG_X = [[y * NX + x for x in range(NX)] for y in range(NY)]
ALONG_Y = [[y * NX + x for y in range(NY)] for x in range(NX)]
TEAM = [[4 * a + 2 * q + c for a in range(NA) for c in range(2)] for q in range(2)]
SAME_CORE = [[4 * a + 2 * q + c for a in range(NA)] for q in range(2) for c in range(2)]
MEMBERS = 4 * NA
BF = jnp.bfloat16
F32 = jnp.float32
VMEM = 16 * 2**20


def swap(x, bit):
    return lax.ppermute(x, "member", [(m, m ^ bit) for m in range(MEMBERS)])


def exchange(x, groups):
    return lax.all_to_all(
        x, "member", split_axis=0, concat_axis=0, tiled=True, axis_index_groups=groups
    )


def parts_kernel(which_ref, x_ref, w_ref, out_ref):
    out_ref[0] = jnp.dot(w_ref[...], x_ref[0, 0], preferred_element_type=F32).astype(BF)


def parts(which, routed, weights):
    na, _, depth, slots = routed.shape
    ff = weights.shape[0]
    return pl.pallas_call(
        parts_kernel,
        grid_spec=pltpu.PrefetchScalarGridSpec(
            num_scalar_prefetch=1,
            grid=(na,),
            in_specs=[
                pl.BlockSpec((1, 1, depth, slots), lambda i, which: (i, which[0], 0, 0)),
                pl.BlockSpec((ff, depth), lambda i, which: (0, 0)),
            ],
            out_specs=pl.BlockSpec((1, ff, slots), lambda i, which: (i, 0, 0)),
        ),
        out_shape=jax.ShapeDtypeStruct((na, ff, slots), BF),
        compiler_params=pltpu.CompilerParams(vmem_limit_bytes=VMEM),
        cost_estimate=pl.CostEstimate(
            flops=2 * na * ff * depth * slots,
            bytes_accessed=2 * (na * depth * slots + ff * depth + na * ff * slots),
            transcendentals=0,
        ),
        name="parts",
    )(which, routed, weights)


def hidden_kernel(scale, p_ref, cot_ref, out_ref):
    total = p_ref[0].astype(F32)
    for a in range(1, p_ref.shape[0]):
        total += p_ref[a].astype(F32)
    pre = total.T * scale
    sig = 1.0 / (1.0 + jnp.exp(-pre))
    grad = sig * (1.0 + pre * (1.0 - sig))
    hid = (cot_ref[...].astype(F32) * grad).astype(BF)
    for a in range(out_ref.shape[0]):
        out_ref[a] = hid


def hidden(partial, cot, scale):
    na, ff, slots = partial.shape
    blk = 256
    return pl.pallas_call(
        lambda *refs: hidden_kernel(scale, *refs),
        grid=(ff // blk,),
        in_specs=[
            pl.BlockSpec((na, blk, slots), lambda i: (0, i, 0)),
            pl.BlockSpec((slots, blk), lambda i: (0, i)),
        ],
        out_specs=pl.BlockSpec((na, slots, blk), lambda i: (0, 0, i)),
        out_shape=jax.ShapeDtypeStruct((na, slots, ff), BF),
        compiler_params=pltpu.CompilerParams(vmem_limit_bytes=VMEM),
        name="hidden",
    )(partial, cot)


def grad_kernel(which_ref, xm_ref, xo_ref, hm_ref, ho_ref, out_ref, acc_ref):
    step = pl.program_id(0)
    left = jnp.concatenate([xm_ref[0, 0, 0], xo_ref[0, 0, 0]], axis=1)
    right = jnp.concatenate([hm_ref[0], ho_ref[0]], axis=0)
    part = jnp.dot(left, right, preferred_element_type=F32)

    @pl.when(step == 0)
    def _():
        acc_ref[...] = part

    @pl.when(step > 0)
    def _():
        acc_ref[...] += part

    @pl.when(step == pl.num_programs(0) - 1)
    def _():
        out_ref[...] = acc_ref[...].astype(out_ref.dtype)


def team_grad(which, block, routed, hid_mine, hid_other, dtype):
    na, _, _, rows, slots = routed.shape
    ff = hid_mine.shape[2]
    return pl.pallas_call(
        grad_kernel,
        grid_spec=pltpu.PrefetchScalarGridSpec(
            num_scalar_prefetch=1,
            grid=(na,),
            in_specs=[
                pl.BlockSpec((1, 1, 1, rows, slots), lambda i, w: (i, w[0], block, 0, 0)),
                pl.BlockSpec((1, 1, 1, rows, slots), lambda i, w: (i, 1 - w[0], block, 0, 0)),
                pl.BlockSpec((1, slots, ff), lambda i, w: (i, 0, 0)),
                pl.BlockSpec((1, slots, ff), lambda i, w: (i, 0, 0)),
            ],
            out_specs=pl.BlockSpec((rows, ff), lambda i, w: (0, 0)),
            scratch_shapes=[pltpu.VMEM((rows, ff), F32)],
        ),
        out_shape=jax.ShapeDtypeStruct((rows, ff), dtype),
        compiler_params=pltpu.CompilerParams(vmem_limit_bytes=VMEM),
        cost_estimate=pl.CostEstimate(
            flops=4 * na * rows * slots * ff,
            bytes_accessed=4 * na * slots * (rows + ff) + 4 * rows * ff,
            transcendentals=0,
        ),
        name="team_grad",
    )(which, routed, routed, hid_mine, hid_other)


def step_kernel(scale, own_ref, far_ref, m1_ref, m2_ref, err_ref, out_ref):
    grad = (own_ref[...] + far_ref[...].astype(F32)) * scale
    one = 0.9 * m1_ref[...] + 0.1 * grad
    two = 0.95 * m2_ref[...] + 0.05 * grad * grad
    moved = 0.25 * (one / (jnp.sqrt(two) + 1e-08)) + err_ref[...].astype(F32)
    out_ref[...] = moved.T.astype(BF)


def inner_step(own, far, m1, m2, err, scale):
    rows, ff = own.shape
    blk = 256
    spec = pl.BlockSpec((rows, blk), lambda i: (0, i))
    return pl.pallas_call(
        lambda *refs: step_kernel(scale, *refs),
        grid=(ff // blk,),
        in_specs=[spec] * 5,
        out_specs=pl.BlockSpec((blk, rows), lambda i: (i, 0)),
        out_shape=jax.ShapeDtypeStruct((ff, rows), BF),
        compiler_params=pltpu.CompilerParams(vmem_limit_bytes=VMEM),
        name="inner_step",
    )(own, far, m1, m2, err)


def local(
    tokens,
    cotangent,
    slot_token,
    outer_weight,
    outer_momentum,
    first_moment,
    second_moment,
    error_state,
):
    scale = float(tokens.shape[2]) ** (-0.5)
    rows, cols = outer_weight.shape
    slots = slot_token.shape[1]
    weight_t = outer_weight.T
    member = lax.axis_index("member")
    core = member & 1
    q = (member >> 1) & 1
    mine = core.astype(jnp.int32).reshape(1)
    other = 1 - mine

    chosen = lax.broadcasted_iota(jnp.int32, (tokens.shape[1], slots), 0) == slot_token
    picked = lax.dot_general(
        tokens[0],
        chosen.astype(BF),
        (((0,), (0,)), ((), ())),
        preferred_element_type=F32,
    ).astype(BF)
    picked = picked.reshape(NA, 2, 2, rows, slots)
    near = lax.dynamic_index_in_dim(picked, q, axis=1, keepdims=False)
    far = lax.dynamic_index_in_dim(picked, 1 - q, axis=1, keepdims=False)
    picked = jnp.stack([near, far], axis=2).reshape(2 * NA, 2 * rows, slots)
    low = weight_t.astype(BF)
    low = jnp.concatenate([low, swap(low, 2)], axis=1)
    picked, low = lax.optimization_barrier((picked, low))
    routed = exchange(picked, TEAM).reshape(NA, 2, 2 * rows, slots)
    low = lax.all_gather(low, "island", axis=0, tiled=True, axis_index_groups=ALONG_X)
    weights = lax.all_gather(low, "island", axis=0, tiled=True, axis_index_groups=ALONG_Y)

    sent = swap(parts(other, routed, weights), 1)
    kept = parts(mine, routed, weights)
    summed = (kept.astype(F32) + sent.astype(F32)).astype(BF)
    hid = hidden(exchange(summed, SAME_CORE), cotangent[0], scale)
    hid_mine = exchange(hid, SAME_CORE)
    hid_other = swap(hid_mine, 1)

    routed = routed.reshape(NA, 2, 2, rows, slots)
    far = swap(team_grad(mine, 1, routed, hid_mine, hid_other, BF), 2)
    own = team_grad(mine, 0, routed, hid_mine, hid_other, F32)
    moved = inner_step(own, far, first_moment[0], second_moment[0], error_state[0], scale)
    shares = lax.all_to_all(
        moved.reshape(NX * NY, cols, rows), "island", split_axis=0, concat_axis=0, tiled=True
    )
    averaged = jnp.sum(shares.astype(F32), axis=0) / float(NX * NY) + 0.025 * weight_t
    new_momentum = 0.9 * outer_momentum.T + averaged
    new_outer = weight_t - 0.7 * (averaged + 0.9 * new_momentum)
    return (new_outer.T, new_momentum.T)


def solution(mesh):
    in_specs = (
        P("island", "member", None),
        P("island", "member", None),
        P("island", "member"),
        P("member", "island"),
        P("member", "island"),
        P("island", "member", None),
        P("island", "member", None),
        P("island", "member", None),
    )
    out_specs = (P("member", "island"), P("member", "island"))
    return jax.shard_map(local, mesh=mesh, in_specs=in_specs, out_specs=out_specs, check_vma=False)
```

time: 358 us -> 173 us (0.48)
  the two profiles are of different devices: /device:TPU:16 before, /device:TPU:8 now
where the time goes in v2:
time: 173 us
  blocking collectives  121 us (70%)
  starting transfers between devices  19.6 us (11%)
  waiting for transfers between devices  14.4 us (8%)
  Pallas kernels  8.68 us (5%)
  local copies, waits for them, and re-layouts  4.3 us (2%)
  matrix products  2.3 us (1%)
  other arithmetic  2.05 us (1%)
    all_to_all x2, blocking collectives, exchange(): lax.all_to_all(x, 'member', split_axis=0, concat_axis=0, tiled=True, axis...  52.6 us
    all_gather x1, blocking collectives, local(): lax.all_gather(low, 'island', axis=0, tiled=True, axis_index_groups=ALONG_Y)  29.3 us
    all_to_all x1, blocking collectives, local(): lax.all_to_all(moved.reshape(NX * NY, cols, rows), 'island', split_axis=0...  26.6 us
    ppermute x4, waiting for transfers between devices, swap(): return lax.ppermute(x, 'member', [(m, m ^ bit) for m in range(MEMBERS)])  14.3 us
    all_gather x1, blocking collectives, local(): lax.all_gather(low, 'island', axis=0, tiled=True, axis_index_groups=ALONG_X)  12.3 us
    ppermute x4, starting transfers between devices, swap(): return lax.ppermute(x, 'member', [(m, m ^ bit) for m in range(MEMBERS)])  10.2 us
    all_to_all x1, starting transfers between devices, exchange(): lax.all_to_all(x, 'member', split_axis=0, concat_axis=0, tiled=True, axis...  9.41 us
    pallas_call x2, Pallas kernels, parts(): pl.pallas_call(parts_kernel, grid_spec=pltpu.PrefetchScalarGridSpec(num_s...  3.51 us
  transfers between devices with their start and end apart: 5, of which 3 were waited for; matrix products, arithmetic and copies ran while one was open for 3% of the time, Pallas kernels for 2%

profile of v2, /device:TPU:8, one launch (start us, length us, event | category | flops | bytes accessed | tf_op | source)
XLA Modules:
  0.0 172.9 jit_solution(16727473456349819121)
XLA Ops:
  0.6 0.0 copy-start
  0.6 0.9 convert_bitcast_fusion
  1.5 4.3 %collective-permute-start = (bf16[24,320]{1,0:T(8,128)(2,1)S(1)}, bf16[24,320]{1,0:T(8,128)(2,1)S(1)}, u32[]{:S(2)}, u32[]{:S(2)}) collective-permute-start(bf16[24,320]{1,0:T(8,128)(2,1)S(1)} %convert_bitcast_fusion), channel_id=1, source_target_pairs={{0,2},{1,3},{2,0},{3,1},{4,6},{5,7},{6,4},{7,5},{8,10},{9,11},{10,... | collective-permute-start | bytes 46088 | tf_op jit(solution)/shard_map/ppermute | solution.py:20
  5.8 0.0 copy-done
  5.8 2.3 %fusion = bf16[5120,128]{0,1:T(8,128)(2,1)} fusion(bf16[1,144,5120]{2,1,0:T(8,128)(2,1)S(1)} %copy-done, s32[128]{0:T(128)} %bitcast.42), kind=kOutput, calls=%fused_computation.1 | convolution fusion | flops 189417472 | bytes 2785792 | tf_op jit(solution)/shard_map/dot_general | solution.py:178
  8.1 1.8 %copy.11 = bf16[5120,128]{1,0:T(8,128)(2,1)S(1)} copy(bf16[5120,128]{0,1:T(8,128)(2,1)} %fusion) | data formatting | bytes 2621440 | tf_op jit(solution)/shard_map/convert_element_type | solution.py:183
  9.9 0.1 dynamic-slice_bitcast_fusion.1
  10.0 0.1 pad_maximum_fusion
  10.1 1.2 copy.12
  11.3 0.0 collective-permute-done
  11.3 0.1 pad_maximum_fusion.1
  11.4 9.4 %all-to-all-start = ((bf16[8,640,128]{2,1,0:T(8,128)(2,1)}), bf16[8,640,128]{2,1,0:T(8,128)(2,1)S(1)}, u32[]{:S(2)}, u32[]{:S(2)}) async-start(bf16[8,640,128]{2,1,0:T(8,128)(2,1)} %bitcast.40), calls=%async_computation | async-start | bytes 2621440 | tf_op jit(solution)/shard_map/all_to_all | solution.py:24
  20.8 12.3 %all_gather.6 = bf16[96,640]{1,0:T(8,128)(2,1)S(1)} all-gather(bf16[24,640]{1,0:T(8,128)(2,1)S(1)} %pad_maximum_fusion.1), channel_id=1, replica_groups={{0,16,32,48},{64,80,96,112},{128,144,160,176},{192,208,224,240},{256,27..., dimensions={0}, use_global_device_ids=true | all-gather | bytes 153600 | tf_op jit(solution)/shard_map/all_gather | solution.py:192
  33.1 29.3 %all_gather.7.w_ref = bf16[768,640]{1,0:T(8,128)(2,1)} all-gather(bf16[96,640]{1,0:T(8,128)(2,1)S(1)} %all_gather.6), channel_id=1, replica_groups={{0,64,128,192,256,320,384,448},{16,80,144,208,272,336,400,464},{32,96,1..., dimensions={0}, use_global_device_ids=true | all-gather | bytes 1105920 | tf_op jit(solution)/shard_map/all_gather | solution.py:193
  62.5 0.0 all-to-all-done
  62.5 0.0 copy-start.1
  62.5 1.2 copy-done.1
  63.7 1.7 %parts.3 = bf16[4,768,128]{2,1,0:T(8,128)(2,1)S(1)} custom-call(s32[1]{0:T(128)S(6)} %sub.11.which_ref, bf16[4,2,640,128]{3,2,1,0:T(8,128)(2,1)S(1)} %bitcast.29, bf16[768,640]{1,0:T(8,128)(2,1)S(1)} %copy-done.1), custom_call_target="tpu_custom_call" | custom-call | flops 503316480 | bytes 2424832 | tf_op jit(solution)/shard_map/parts/pallas_call | solution.py:36
  65.4 1.9 %collective-permute-start.1 = (bf16[4,768,128]{2,1,0:T(8,128)(2,1)S(1)}, bf16[4,768,128]{2,1,0:T(8,128)(2,1)S(1)}, u32[]{:S(2)}, u32[]{:S(2)}) collective-permute-start(bf16[4,768,128]{2,1,0:T(8,128)(2,1)S(1)} %parts.3), channel_id=1, source_target_pairs={{0,1},{1,0},{2,3},{3,2},{4,5},{5,4},{6,7},{7,6},{8,9},{9,8},{10,11... | collective-permute-start | bytes 2359304 | tf_op jit(solution)/shard_map/ppermute | solution.py:20
  67.3 1.8 %parts.2 = bf16[4,768,128]{2,1,0:T(8,128)(2,1)S(1)} custom-call(s32[1]{0:T(128)} %bitcast.which_ref, bf16[4,2,640,128]{3,2,1,0:T(8,128)(2,1)S(1)} %bitcast.30, bf16[768,640]{1,0:T(8,128)(2,1)S(1)} %copy-done.1), custom_call_target="tpu_custom_call" | custom-call | flops 503316480 | bytes 2424832 | tf_op jit(solution)/shard_map/parts/pallas_call | solution.py:36
  69.1 0.5 collective-permute-done.1
  69.6 0.2 add_convert_fusion
  69.8 0.0 copy-start.5
  69.8 29.6 %all_to_all.20.refs_0_ = bf16[4,768,128]{2,1,0:T(8,128)(2,1)S(1)} all-to-all(bf16[4,768,128]{2,1,0:T(8,128)(2,1)S(1)} %add_convert_fusion), channel_id=1, replica_groups={{0,4,8,12},{1,5,9,13},{2,6,10,14},{3,7,11,15},{16,20,24,28},{17,21,25,2..., dimensions={0} | all-to-all | bytes 1572864 | tf_op jit(solution)/shard_map/all_to_all | solution.py:24
  99.4 0.0 copy-done.5
  99.4 0.6 hidden.1
  100.0 23.0 %all_to_all.21.hm_ref = bf16[4,128,768]{2,1,0:T(8,128)(2,1)S(1)} all-to-all(bf16[4,128,768]{2,1,0:T(8,128)(2,1)S(1)} %hidden.1), channel_id=1, replica_groups={{0,4,8,12},{1,5,9,13},{2,6,10,14},{3,7,11,15},{16,20,24,28},{17,21,25,2..., dimensions={0} | all-to-all | bytes 1572864 | tf_op jit(solution)/shard_map/all_to_all | solution.py:24
  123.0 1.9 %collective-permute-start.2 = (bf16[4,128,768]{2,1,0:T(8,128)(2,1)S(1)}, bf16[4,128,768]{2,1,0:T(8,128)(2,1)S(1)}, u32[]{:S(2)}, u32[]{:S(2)}) collective-permute-start(bf16[4,128,768]{2,1,0:T(8,128)(2,1)S(1)} %all_to_all.21.hm_ref), channel_id=1, source_target_pairs={{0,1},{1,0},{2,3},{3,2},{4,5},{5,4},{6,7},{7,6},{8,9},{9,8},{10,11... | collective-permute-start | bytes 2359304 | tf_op jit(solution)/shard_map/ppermute | solution.py:20
  124.9 2.3 %collective-permute-done.2.ho_ref = bf16[4,128,768]{2,1,0:T(8,128)(2,1)S(1)} collective-permute-done((bf16[4,128,768]{2,1,0:T(8,128)(2,1)S(1)}, bf16[4,128,768]{2,1,0:T(8,128)(2,1)S(1)}, u32[]{:S(2)}, u32[]{:S(2)}) %collective-permute-start.2) | collective-permute-done | bytes 786464 | tf_op jit(solution)/shard_map/ppermute | solution.py:20
  127.2 1.6 team_grad.3
  128.8 0.0 copy-start.2
  128.8 0.0 copy-start.3
  128.8 0.0 copy-start.4
  128.8 2.1 %collective-permute-start.3 = (bf16[320,768]{1,0:T(8,128)(2,1)S(1)}, bf16[320,768]{1,0:T(8,128)(2,1)S(1)}, u32[]{:S(2)}, u32[]{:S(2)}) collective-permute-start(bf16[320,768]{1,0:T(8,128)(2,1)S(1)} %team_grad.3), channel_id=1, source_target_pairs={{0,2},{1,3},{2,0},{3,1},{4,6},{5,7},{6,4},{7,5},{8,10},{9,11},{10,... | collective-permute-start | bytes 1474568 | tf_op jit(solution)/shard_map/ppermute | solution.py:20
  130.9 1.6 team_grad.2.refs_0_
  132.5 11.6 %collective-permute-done.3.refs_1_ = bf16[320,768]{1,0:T(8,128)(2,1)S(1)} collective-permute-done((bf16[320,768]{1,0:T(8,128)(2,1)S(1)}, bf16[320,768]{1,0:T(8,128)(2,1)S(1)}, u32[]{:S(2)}, u32[]{:S(2)}) %collective-permute-start.3) | collective-permute-done | bytes 491552 | tf_op jit(solution)/shard_map/ppermute | solution.py:20
  144.1 0.0 copy-done.2
  144.1 0.0 copy-done.3
  144.1 0.0 copy-done.4
  144.1 1.4 inner_step.1
  145.5 0.0 copy-start.6
  145.5 0.0 copy-start.7
  145.5 26.6 %all_to_all.22 = bf16[32,24,320]{2,1,0:T(8,128)(2,1)S(1)} all-to-all(bf16[32,24,320]{2,1,0:T(8,128)(2,1)S(1)} %bitcast.35), channel_id=1, replica_groups=mesh['island'=32,'member'=16] {'island'}, dimensions={0} | all-to-all | bytes 983040 | tf_op jit(solution)/shard_map/all_to_all | solution.py:206
  172.1 0.1 convert_reduce_fusion
  172.2 0.0 copy-done.6
  172.2 0.0 copy-done.7
  172.2 0.6 multiply_subtract_fusion
Async XLA Ops:
  0.6 5.2 %copy-start = (bf16[1,144,5120]{2,1,0:T(8,128)(2,1)S(1)}, bf16[1,144,5120]{2,1,0:T(8,128)(2,1)}, u32[]{:S(2)}) copy-start(bf16[1,144,5120]{2,1,0:T(8,128)(2,1)} %param.8) | copy-start | bytes 4423684
  1.5 9.8 %collective-permute-start = (bf16[24,320]{1,0:T(8,128)(2,1)S(1)}, bf16[24,320]{1,0:T(8,128)(2,1)S(1)}, u32[]{:S(2)}, u32[]{:S(2)}) collective-permute-start(bf16[24,320]{1,0:T(8,128)(2,1)S(1)} %convert_bitcast_fusion), channel_id=1, source_target_pairs={{0,2},{1,3},{2,0},{3,1},{4,6},{5,7},{6,4},{7,5},{8,10},{9,11},{10,... | collective-permute-start | bytes 46088 | tf_op jit(solution)/shard_map/ppermute | solution.py:20
  11.4 51.1 %all-to-all-start = ((bf16[8,640,128]{2,1,0:T(8,128)(2,1)}), bf16[8,640,128]{2,1,0:T(8,128)(2,1)S(1)}, u32[]{:S(2)}, u32[]{:S(2)}) async-start(bf16[8,640,128]{2,1,0:T(8,128)(2,1)} %bitcast.40), calls=%async_computation | async-start | bytes 2621440 | tf_op jit(solution)/shard_map/all_to_all | solution.py:24
  62.5 1.2 copy-start.1
  65.4 4.2 %collective-permute-start.1 = (bf16[4,768,128]{2,1,0:T(8,128)(2,1)S(1)}, bf16[4,768,128]{2,1,0:T(8,128)(2,1)S(1)}, u32[]{:S(2)}, u32[]{:S(2)}) collective-permute-start(bf16[4,768,128]{2,1,0:T(8,128)(2,1)S(1)} %parts.3), channel_id=1, source_target_pairs={{0,1},{1,0},{2,3},{3,2},{4,5},{5,4},{6,7},{7,6},{8,9},{9,8},{10,11... | collective-permute-start | bytes 2359304 | tf_op jit(solution)/shard_map/ppermute | solution.py:20
  69.8 29.6 %copy-start.5 = (bf16[1,128,768]{2,1,0:T(8,128)(2,1)S(1)}, bf16[1,128,768]{2,1,0:T(8,128)(2,1)}, u32[]{:S(2)}) copy-start(bf16[1,128,768]{2,1,0:T(8,128)(2,1)} %param.9) | copy-start | bytes 589828
  123.0 4.2 %collective-permute-start.2 = (bf16[4,128,768]{2,1,0:T(8,128)(2,1)S(1)}, bf16[4,128,768]{2,1,0:T(8,128)(2,1)S(1)}, u32[]{:S(2)}, u32[]{:S(2)}) collective-permute-start(bf16[4,128,768]{2,1,0:T(8,128)(2,1)S(1)} %all_to_all.21.hm_ref), channel_id=1, source_target_pairs={{0,1},{1,0},{2,3},{3,2},{4,5},{5,4},{6,7},{7,6},{8,9},{9,8},{10,11... | collective-permute-start | bytes 2359304 | tf_op jit(solution)/shard_map/ppermute | solution.py:20
  128.8 15.3 %copy-start.2 = (f32[1,320,768]{2,1,0:T(8,128)S(1)}, f32[1,320,768]{2,1,0:T(8,128)}, u32[]{:S(2)}) copy-start(f32[1,320,768]{2,1,0:T(8,128)} %param.13) | copy-start | bytes 2949124
  128.8 15.3 %copy-start.3 = (f32[1,320,768]{2,1,0:T(8,128)S(1)}, f32[1,320,768]{2,1,0:T(8,128)}, u32[]{:S(2)}) copy-start(f32[1,320,768]{2,1,0:T(8,128)} %param.14) | copy-start | bytes 2949124
  128.8 15.3 %copy-start.4 = (bf16[1,320,768]{2,1,0:T(8,128)(2,1)S(1)}, bf16[1,320,768]{2,1,0:T(8,128)(2,1)}, u32[]{:S(2)}) copy-start(bf16[1,320,768]{2,1,0:T(8,128)(2,1)} %param.15) | copy-start | bytes 1474564
  128.8 15.3 %collective-permute-start.3 = (bf16[320,768]{1,0:T(8,128)(2,1)S(1)}, bf16[320,768]{1,0:T(8,128)(2,1)S(1)}, u32[]{:S(2)}, u32[]{:S(2)}) collective-permute-start(bf16[320,768]{1,0:T(8,128)(2,1)S(1)} %team_grad.3), channel_id=1, source_target_pairs={{0,2},{1,3},{2,0},{3,1},{4,6},{5,7},{6,4},{7,5},{8,10},{9,11},{10,... | collective-permute-start | bytes 1474568 | tf_op jit(solution)/shard_map/ppermute | solution.py:20
  145.5 26.7 %copy-start.6 = (f32[320,24]{0,1:T(8,128)S(1)}, f32[320,24]{0,1:T(8,128)}, u32[]{:S(2)}) copy-start(f32[320,24]{0,1:T(8,128)} %param.11) | copy-start | bytes 92164
  145.5 26.7 %copy-start.7 = (f32[320,24]{0,1:T(8,128)S(1)}, f32[320,24]{0,1:T(8,128)}, u32[]{:S(2)}) copy-start(f32[320,24]{0,1:T(8,128)} %param.12) | copy-start | bytes 92164

commit v3 on v2

--- a/solution.py
+++ b/solution.py
@@ -7,13 +7,13 @@
 
 NY, NX, NA = 8, 4, 4
 ALONG_X = [[y * NX + x for x in range(NX)] for y in range(NY)]
-ALONG_Y = [[y * NX + x for y in range(NY)] for x in range(NX)]
 TEAM = [[4 * a + 2 * q + c for a in range(NA) for c in range(2)] for q in range(2)]
 SAME_CORE = [[4 * a + 2 * q + c for a in range(NA)] for q in range(2) for c in range(2)]
 MEMBERS = 4 * NA
 BF = jnp.bfloat16
 F32 = jnp.float32
 VMEM = 16 * 2**20
+PACKED = 64
 
 
 def swap(x, bit):
@@ -24,6 +24,37 @@
     return lax.all_to_all(
         x, "member", split_axis=0, concat_axis=0, tiled=True, axis_index_groups=groups
     )
+
+
+def pick_kernel(q_ref, tok_ref, slot_ref, out_ref):
+    shape = (tok_ref.shape[0], slot_ref.shape[1])
+    chosen = (lax.broadcasted_iota(jnp.int32, shape, 0) == slot_ref[...]).astype(BF)
+    got = lax.dot_general(
+        tok_ref[...], chosen, (((0,), (0,)), ((), ())), preferred_element_type=F32
+    )
+    out_ref[...] = got.astype(BF).reshape(out_ref.shape)
+
+
+def pick(q, tokens, slot_token, rows):
+    slots = slot_token.shape[1]
+    return pl.pallas_call(
+        pick_kernel,
+        grid_spec=pltpu.PrefetchScalarGridSpec(
+            num_scalar_prefetch=1,
+            grid=(NA, 2),
+            in_specs=[
+                pl.BlockSpec(
+                    (tokens.shape[0], 2 * rows),
+                    lambda i, j, q: (0, 2 * i + q[0] + j - 2 * q[0] * j),
+                ),
+                pl.BlockSpec((1, slots), lambda i, j, q: (0, 0)),
+            ],
+            out_specs=pl.BlockSpec((1, 2, 1, rows, slots), lambda i, j, q: (i, 0, j, 0, 0)),
+        ),
+        out_shape=jax.ShapeDtypeStruct((NA, 2, 2, rows, slots), BF),
+        compiler_params=pltpu.CompilerParams(vmem_limit_bytes=VMEM),
+        name="pick",
+    )(q, tokens, slot_token).reshape(2 * NA, 2 * rows, slots)
 
 
 def parts_kernel(which_ref, x_ref, w_ref, out_ref):
@@ -59,6 +90,9 @@
     total = p_ref[0].astype(F32)
     for a in range(1, p_ref.shape[0]):
         total += p_ref[a].astype(F32)
+    ff, slots = total.shape
+    total = total.reshape(NX, NY, ff // (NX * NY), slots)
+    total = jnp.concatenate([total[x, y] for y in range(NY) for x in range(NX)], axis=0)
     pre = total.T * scale
     sig = 1.0 / (1.0 + jnp.exp(-pre))
     grad = sig * (1.0 + pre * (1.0 - sig))
@@ -69,15 +103,10 @@
 
 def hidden(partial, cot, scale):
     na, ff, slots = partial.shape
-    blk = 256
     return pl.pallas_call(
         lambda *refs: hidden_kernel(scale, *refs),
-        grid=(ff // blk,),
-        in_specs=[
-            pl.BlockSpec((na, blk, slots), lambda i: (0, i, 0)),
-            pl.BlockSpec((slots, blk), lambda i: (0, i)),
-        ],
-        out_specs=pl.BlockSpec((na, slots, blk), lambda i: (0, 0, i)),
+        in_specs=[pl.BlockSpec(memory_space=pltpu.VMEM)] * 2,
+        out_specs=pl.BlockSpec(memory_space=pltpu.VMEM),
         out_shape=jax.ShapeDtypeStruct((na, slots, ff), BF),
         compiler_params=pltpu.CompilerParams(vmem_limit_bytes=VMEM),
         name="hidden",
@@ -131,24 +160,43 @@
     )(which, routed, routed, hid_mine, hid_other)
 
 
-def step_kernel(scale, own_ref, far_ref, m1_ref, m2_ref, err_ref, out_ref):
+def pack(x):
+    tail = x[:, :, 256:]
+    pad = jnp.zeros_like(tail[:, :8])
+    return jnp.concatenate(
+        [
+            x[:, :, :128],
+            x[:, :, 128:256],
+            jnp.concatenate([tail[:, :8], tail[:, 8:16]], axis=2),
+            jnp.concatenate([tail[:, 16:], pad], axis=2),
+        ],
+        axis=1,
+    )
+
+
+def unpack(x):
+    tail = jnp.concatenate([x[48:56, :64], x[48:56, 64:], x[56:, :64]], axis=0)
+    return jnp.concatenate([x[:24], x[24:48], tail], axis=1)
+
+
+def step_kernel(scale, cols, own_ref, far_ref, m1_ref, m2_ref, err_ref, out_ref):
     grad = (own_ref[...] + far_ref[...].astype(F32)) * scale
     one = 0.9 * m1_ref[...] + 0.1 * grad
     two = 0.95 * m2_ref[...] + 0.05 * grad * grad
     moved = 0.25 * (one / (jnp.sqrt(two) + 1e-08)) + err_ref[...].astype(F32)
-    out_ref[...] = moved.T.astype(BF)
-
-
-def inner_step(own, far, m1, m2, err, scale):
+    out_ref[...] = pack(moved.T.reshape(-1, cols, moved.shape[0])).astype(BF)
+
+
+def inner_step(own, far, m1, m2, err, scale, cols):
     rows, ff = own.shape
-    blk = 256
+    blk = ff // 2
     spec = pl.BlockSpec((rows, blk), lambda i: (0, i))
     return pl.pallas_call(
-        lambda *refs: step_kernel(scale, *refs),
+        lambda *refs: step_kernel(scale, cols, *refs),
         grid=(ff // blk,),
         in_specs=[spec] * 5,
-        out_specs=pl.BlockSpec((blk, rows), lambda i: (i, 0)),
-        out_shape=jax.ShapeDtypeStruct((ff, rows), BF),
+        out_specs=pl.BlockSpec((blk // cols, PACKED, 128), lambda i: (i, 0, 0)),
+        out_shape=jax.ShapeDtypeStruct((ff // cols, PACKED, 128), BF),
         compiler_params=pltpu.CompilerParams(vmem_limit_bytes=VMEM),
         name="inner_step",
     )(own, far, m1, m2, err)
@@ -174,23 +222,29 @@
     mine = core.astype(jnp.int32).reshape(1)
     other = 1 - mine
 
-    chosen = lax.broadcasted_iota(jnp.int32, (tokens.shape[1], slots), 0) == slot_token
-    picked = lax.dot_general(
-        tokens[0],
-        chosen.astype(BF),
-        (((0,), (0,)), ((), ())),
-        preferred_element_type=F32,
-    ).astype(BF)
-    picked = picked.reshape(NA, 2, 2, rows, slots)
-    near = lax.dynamic_index_in_dim(picked, q, axis=1, keepdims=False)
-    far = lax.dynamic_index_in_dim(picked, 1 - q, axis=1, keepdims=False)
-    picked = jnp.stack([near, far], axis=2).reshape(2 * NA, 2 * rows, slots)
+    picked = pick(q.reshape(1), tokens[0], slot_token, rows)
+
     low = weight_t.astype(BF)
     low = jnp.concatenate([low, swap(low, 2)], axis=1)
     picked, low = lax.optimization_barrier((picked, low))
+    near = lax.ppermute(low, "island", [(i, i ^ NX) for i in range(NX * NY)])
     routed = exchange(picked, TEAM).reshape(NA, 2, 2 * rows, slots)
-    low = lax.all_gather(low, "island", axis=0, tiled=True, axis_index_groups=ALONG_X)
-    weights = lax.all_gather(low, "island", axis=0, tiled=True, axis_index_groups=ALONG_Y)
+    y = lax.axis_index("island") >> 2
+    odd = (y & 1) == 1
+    pair = jnp.where(odd, jnp.stack([near, low]), jnp.stack([low, near]))
+    ring = [pair] + [
+        lax.ppermute(
+            pair,
+            "island",
+            [(i, (i + 2 * NX * k) % (NX * NY)) for i in range(NX * NY)],
+        )
+        for k in (1, 2, 3)
+    ]
+    ring = jnp.stack([ring[k] for k in (0, 3, 2, 1, 0, 3, 2, 1)])
+    column = lax.dynamic_slice_in_dim(ring, (4 - (y >> 1)) & 3, 4, axis=0)
+    weights = lax.all_gather(
+        column.reshape(NY * cols, 2 * rows), "island", axis=0, tiled=True, axis_index_groups=ALONG_X
+    )
 
     sent = swap(parts(other, routed, weights), 1)
     kept = parts(mine, routed, weights)
@@ -202,11 +256,11 @@
     routed = routed.reshape(NA, 2, 2, rows, slots)
     far = swap(team_grad(mine, 1, routed, hid_mine, hid_other, BF), 2)
     own = team_grad(mine, 0, routed, hid_mine, hid_other, F32)
-    moved = inner_step(own, far, first_moment[0], second_moment[0], error_state[0], scale)
+    moved = inner_step(own, far, first_moment[0], second_moment[0], error_state[0], scale, cols)
     shares = lax.all_to_all(
-        moved.reshape(NX * NY, cols, rows), "island", split_axis=0, concat_axis=0, tiled=True
-    )
-    averaged = jnp.sum(shares.astype(F32), axis=0) / float(NX * NY) + 0.025 * weight_t
+        moved, "island", split_axis=0, concat_axis=0, tiled=True
+    )
+    averaged = unpack(jnp.sum(shares.astype(F32), axis=0)) / float(NX * NY) + 0.025 * weight_t
     new_momentum = 0.9 * outer_momentum.T + averaged
     new_outer = weight_t - 0.7 * (averaged + 0.9 * new_momentum)
     return (new_outer.T, new_momentum.T)

time: 173 us -> 168 us (0.971)
  blocking collectives: 121 us -> 92.1 us
  starting transfers between devices: 19.6 us -> 36.7 us
  waiting for transfers between devices: 14.4 us -> 20.6 us
  Pallas kernels: 8.68 us -> 12.8 us
  matrix products: 2.3 us -> 0 us
  local copies, waits for them, and re-layouts: 4.3 us -> 2.25 us
    all_gather x2 -> x1, blocking collectives: 41.7 us -> 15.4 us  [local(): lax.all_gather(column.reshape(NY * cols, 2 * rows), 'island', axis=0, til...]
    ppermute x0 -> x4, starting transfers between devices: none -> 17.1 us  [the longest x3 14.8 us: local(): lax.ppermute(pair, 'island', [(i, (i + 2 * NX * k) % (NX * NY)) for i in...]
    ppermute x0 -> x4, waiting for transfers between devices: none -> 6.27 us  [the longest x1 3.4 us: local(): near = lax.ppermute(low, 'island', [(i, i ^ NX) for i in range(NX * NY)])]
    pallas_call x2 -> x3, Pallas kernels: 1.99 us -> 6.14 us  [the longest x1 4.42 us: pick(): pl.pallas_call(pick_kernel, grid_spec=pltpu.PrefetchScalarGridSpec(num_sc...]
    all_to_all x1, blocking collectives: 26.6 us -> 24.2 us  [local(): lax.all_to_all(moved, 'island', split_axis=0, concat_axis=0, tiled=True)]
    dot_general x1 -> x0, matrix products: 2.3 us -> none  [local(): lax.dot_general(tokens[0], chosen.astype(BF), (((0,), (0,)), ((), ())), p...]
    convert_element_type x1 -> x0, local copies, waits for them, and re-layouts: 1.76 us -> none  [local(): picked = lax.dot_general(tokens[0], chosen.astype(BF), (((0,), (0,)), (()...]
  transfers between devices with their start and end apart: 5 -> 9, of which waited for: 3 -> 5; matrix products, arithmetic and copies ran while one was open for 3% -> 0% of each run, Pallas kernels for 2% -> 5%
where the time goes in v3:
time: 168 us; the launch traced here: 167 us
  blocking collectives  92.1 us (55%)
  starting transfers between devices  36.7 us (22%)
  waiting for transfers between devices  20.6 us (12%)
  Pallas kernels  12.8 us (8%)
  local copies, waits for them, and re-layouts  2.25 us (1%)
  other arithmetic  1.85 us (1%)
    all_to_all x2, blocking collectives, exchange(): lax.all_to_all(x, 'member', split_axis=0, concat_axis=0, tiled=True, axis...  52.5 us
    all_to_all x1, blocking collectives, local(): lax.all_to_all(moved, 'island', split_axis=0, concat_axis=0, tiled=True)  24.2 us
    all_gather x1, blocking collectives, local(): lax.all_gather(column.reshape(NY * cols, 2 * rows), 'island', axis=0, til...  15.4 us
    ppermute x3, starting transfers between devices, local(): lax.ppermute(pair, 'island', [(i, (i + 2 * NX * k) % (NX * NY)) for i in...  14.8 us
    ppermute x4, waiting for transfers between devices, swap(): return lax.ppermute(x, 'member', [(m, m ^ bit) for m in range(MEMBERS)])  14.3 us
    ppermute x4, starting transfers between devices, swap(): return lax.ppermute(x, 'member', [(m, m ^ bit) for m in range(MEMBERS)])  10.2 us
    all_to_all x1, starting transfers between devices, exchange(): lax.all_to_all(x, 'member', split_axis=0, concat_axis=0, tiled=True, axis...  9.4 us
    pallas_call x1, Pallas kernels, pick(): pl.pallas_call(pick_kernel, grid_spec=pltpu.PrefetchScalarGridSpec(num_sc...  4.42 us
  transfers between devices with their start and end apart: 9, of which 5 were waited for; matrix products, arithmetic and copies ran while one was open for 0% of the time, Pallas kernels for 5%

profile of v3, /device:TPU:8, one launch (start us, length us, event | category | flops | bytes accessed | tf_op | source)
XLA Modules:
  0.0 167.2 jit_solution(11166795379309126933)
XLA Ops:
  0.6 0.8 bitcast_convert_fusion
  1.4 4.3 %collective-permute-start = (bf16[24,320]{1,0:T(8,128)(2,1)S(1)}, bf16[24,320]{1,0:T(8,128)(2,1)S(1)}, u32[]{:S(2)}, u32[]{:S(2)}) collective-permute-start(bf16[24,320]{1,0:T(8,128)(2,1)S(1)} %bitcast_convert_fusion), channel_id=1, source_target_pairs={{0,2},{1,3},{2,0},{3,1},{4,6},{5,7},{6,4},{7,5},{8,10},{9,11},{10,... | collective-permute-start | bytes 46088 | tf_op jit(solution)/shard_map/ppermute | solution.py:20
  5.7 0.0 copy-start
  5.7 1.4 copy-done
  7.1 0.0 copy-start.5
  7.1 0.7 copy-done.5
  7.7 4.4 %pick.1 = bf16[4,2,2,320,128]{4,3,2,1,0:T(8,128)(2,1)} custom-call(s32[1]{0:T(128)} %bitcast.2.q_ref, bf16[144,5120]{1,0:T(8,128)(2,1)S(1)} %bitcast.52, s32[1,128]{1,0:T(1,128)S(1)} %copy-done.5), custom_call_target="tpu_custom_call" | custom-call | tf_op jit(solution)/shard_map/pick/pallas_call | solution.py:40
  12.1 0.0 collective-permute-done
  12.1 0.1 pad_maximum_fusion
  12.2 9.4 %all-to-all-start = ((bf16[8,640,128]{2,1,0:T(8,128)(2,1)}), bf16[8,640,128]{2,1,0:T(8,128)(2,1)S(1)}, u32[]{:S(2)}, u32[]{:S(2)}) async-start(bf16[8,640,128]{2,1,0:T(8,128)(2,1)} %bitcast.4), calls=%async_computation | async-start | bytes 2621440 | tf_op jit(solution)/shard_map/all_to_all | solution.py:24
  21.6 2.4 %collective-permute-start.1 = (bf16[24,640]{1,0:T(8,128)(2,1)S(1)}, bf16[24,640]{1,0:T(8,128)(2,1)S(1)}, u32[]{:S(2)}, u32[]{:S(2)}) collective-permute-start(bf16[24,640]{1,0:T(8,128)(2,1)S(1)} %pad_maximum_fusion), channel_id=1, source_target_pairs={{0,64},{16,80},{32,96},{48,112},{64,0},{80,16},{96,32},{112,48},{1... | collective-permute-start | bytes 92168 | tf_op jit(solution)/shard_map/ppermute | solution.py:230
  24.0 3.4 %collective-permute-done.1 = bf16[24,640]{1,0:T(8,128)(2,1)S(1)} collective-permute-done((bf16[24,640]{1,0:T(8,128)(2,1)S(1)}, bf16[24,640]{1,0:T(8,128)(2,1)S(1)}, u32[]{:S(2)}, u32[]{:S(2)}) %collective-permute-start.1) | collective-permute-done | bytes 30752 | tf_op jit(solution)/shard_map/ppermute | solution.py:230
  27.4 4.5 %collective-permute-start.4 = (bf16[2,24,640]{2,1,0:T(8,128)(2,1)S(1)}, bf16[2,24,640]{2,1,0:T(8,128)(2,1)S(1)}, u32[]{:S(2)}, u32[]{:S(2)}) collective-permute-start(bf16[2,24,640]{2,1,0:T(8,128)(2,1)S(1)} %maximum_select_fusion.1), channel_id=1, source_target_pairs={{0,128},{16,144},{32,160},{48,176},{64,192},{80,208},{96,224},{112... | collective-permute-start | bytes 184328 | tf_op jit(solution)/shard_map/ppermute | solution.py:236
  31.9 5.0 %collective-permute-start.3 = (bf16[2,24,640]{2,1,0:T(8,128)(2,1)S(1)}, bf16[2,24,640]{2,1,0:T(8,128)(2,1)S(1)}, u32[]{:S(2)}, u32[]{:S(2)}) collective-permute-start(bf16[2,24,640]{2,1,0:T(8,128)(2,1)S(1)} %maximum_select_fusion.1), channel_id=1, source_target_pairs={{0,256},{16,272},{32,288},{48,304},{64,320},{80,336},{96,352},{112... | collective-permute-start | bytes 184328 | tf_op jit(solution)/shard_map/ppermute | solution.py:236
  37.0 5.3 %collective-permute-start.2 = (bf16[2,24,640]{2,1,0:T(8,128)(2,1)S(1)}, bf16[2,24,640]{2,1,0:T(8,128)(2,1)S(1)}, u32[]{:S(2)}, u32[]{:S(2)}) collective-permute-start(bf16[2,24,640]{2,1,0:T(8,128)(2,1)S(1)} %maximum_select_fusion.1), channel_id=1, source_target_pairs={{0,384},{16,400},{32,416},{48,432},{64,448},{80,464},{96,480},{112... | collective-permute-start | bytes 184328 | tf_op jit(solution)/shard_map/ppermute | solution.py:236
  42.3 2.9 %collective-permute-done.2 = bf16[2,24,640]{2,1,0:T(8,128)(2,1)S(1)} collective-permute-done((bf16[2,24,640]{2,1,0:T(8,128)(2,1)S(1)}, bf16[2,24,640]{2,1,0:T(8,128)(2,1)S(1)}, u32[]{:S(2)}, u32[]{:S(2)}) %collective-permute-start.2) | collective-permute-done | bytes 61472 | tf_op jit(solution)/shard_map/ppermute | solution.py:236
  45.1 0.0 collective-permute-done.3
  45.2 0.0 collective-permute-done.4
  45.3 15.4 %all_gather.3.w_ref = bf16[768,640]{1,0:T(8,128)(2,1)S(1)} all-gather(bf16[192,640]{1,0:T(8,128)(2,1)S(1)} %bitcast.57), channel_id=1, replica_groups={{0,16,32,48},{64,80,96,112},{128,144,160,176},{192,208,224,240},{256,27..., dimensions={0}, use_global_device_ids=true | all-gather | bytes 1228800 | tf_op jit(solution)/shard_map/all_gather | solution.py:245
  60.7 0.0 all-to-all-done
  60.7 1.7 %parts.3 = bf16[4,768,128]{2,1,0:T(8,128)(2,1)S(1)} custom-call(s32[1]{0:T(128)S(6)} %sub.10.which_ref, bf16[4,2,640,128]{3,2,1,0:T(8,128)(2,1)S(1)} %bitcast.46, bf16[768,640]{1,0:T(8,128)(2,1)S(1)} %all_gather.3.w_ref), custom_call_target="tpu_custom_call" | custom-call | flops 503316480 | bytes 2424832 | tf_op jit(solution)/shard_map/parts/pallas_call | solution.py:67
  62.4 1.9 %collective-permute-start.5 = (bf16[4,768,128]{2,1,0:T(8,128)(2,1)S(1)}, bf16[4,768,128]{2,1,0:T(8,128)(2,1)S(1)}, u32[]{:S(2)}, u32[]{:S(2)}) collective-permute-start(bf16[4,768,128]{2,1,0:T(8,128)(2,1)S(1)} %parts.3), channel_id=1, source_target_pairs={{0,1},{1,0},{2,3},{3,2},{4,5},{5,4},{6,7},{7,6},{8,9},{9,8},{10,11... | collective-permute-start | bytes 2359304 | tf_op jit(solution)/shard_map/ppermute | solution.py:20
  64.4 1.8 %parts.2 = bf16[4,768,128]{2,1,0:T(8,128)(2,1)S(1)} custom-call(s32[1]{0:T(128)} %bitcast.1.which_ref, bf16[4,2,640,128]{3,2,1,0:T(8,128)(2,1)S(1)} %bitcast.47, bf16[768,640]{1,0:T(8,128)(2,1)S(1)} %all_gather.3.w_ref), custom_call_target="tpu_custom_call" | custom-call | flops 503316480 | bytes 2424832 | tf_op jit(solution)/shard_map/parts/pallas_call | solution.py:67
  66.1 0.0 copy-start.4
  66.1 0.5 collective-permute-done.5
  66.6 0.2 add_convert_fusion
  66.8 29.1 %all_to_all.20.refs_0_ = bf16[4,768,128]{2,1,0:T(8,128)(2,1)S(1)} all-to-all(bf16[4,768,128]{2,1,0:T(8,128)(2,1)S(1)} %add_convert_fusion), channel_id=1, replica_groups={{0,4,8,12},{1,5,9,13},{2,6,10,14},{3,7,11,15},{16,20,24,28},{17,21,25,2..., dimensions={0} | all-to-all | bytes 1572864 | tf_op jit(solution)/shard_map/all_to_all | solution.py:24
  95.9 0.0 copy-done.4
  95.9 0.3 hidden.1
  96.1 23.5 %all_to_all.21.hm_ref = bf16[4,128,768]{2,1,0:T(8,128)(2,1)S(1)} all-to-all(bf16[4,128,768]{2,1,0:T(8,128)(2,1)S(1)} %hidden.1), channel_id=1, replica_groups={{0,4,8,12},{1,5,9,13},{2,6,10,14},{3,7,11,15},{16,20,24,28},{17,21,25,2..., dimensions={0} | all-to-all | bytes 1572864 | tf_op jit(solution)/shard_map/all_to_all | solution.py:24
  119.6 1.9 %collective-permute-start.6 = (bf16[4,128,768]{2,1,0:T(8,128)(2,1)S(1)}, bf16[4,128,768]{2,1,0:T(8,128)(2,1)S(1)}, u32[]{:S(2)}, u32[]{:S(2)}) collective-permute-start(bf16[4,128,768]{2,1,0:T(8,128)(2,1)S(1)} %all_to_all.21.hm_ref), channel_id=1, source_target_pairs={{0,1},{1,0},{2,3},{3,2},{4,5},{5,4},{6,7},{7,6},{8,9},{9,8},{10,11... | collective-permute-start | bytes 2359304 | tf_op jit(solution)/shard_map/ppermute | solution.py:20
  121.5 2.3 %collective-permute-done.6.ho_ref = bf16[4,128,768]{2,1,0:T(8,128)(2,1)S(1)} collective-permute-done((bf16[4,128,768]{2,1,0:T(8,128)(2,1)S(1)}, bf16[4,128,768]{2,1,0:T(8,128)(2,1)S(1)}, u32[]{:S(2)}, u32[]{:S(2)}) %collective-permute-start.6) | collective-permute-done | bytes 786464 | tf_op jit(solution)/shard_map/ppermute | solution.py:20
  123.8 1.6 team_grad.3
  125.4 0.0 copy-start.1
  125.4 0.0 copy-start.2
  125.4 0.0 copy-start.3
  125.4 2.1 %collective-permute-start.7 = (bf16[320,768]{1,0:T(8,128)(2,1)S(1)}, bf16[320,768]{1,0:T(8,128)(2,1)S(1)}, u32[]{:S(2)}, u32[]{:S(2)}) collective-permute-start(bf16[320,768]{1,0:T(8,128)(2,1)S(1)} %team_grad.3), channel_id=1, source_target_pairs={{0,2},{1,3},{2,0},{3,1},{4,6},{5,7},{6,4},{7,5},{8,10},{9,11},{10,... | collective-permute-start | bytes 1474568 | tf_op jit(solution)/shard_map/ppermute | solution.py:20
  127.5 1.6 team_grad.2.refs_0_
  129.1 11.6 %collective-permute-done.7.refs_1_ = bf16[320,768]{1,0:T(8,128)(2,1)S(1)} collective-permute-done((bf16[320,768]{1,0:T(8,128)(2,1)S(1)}, bf16[320,768]{1,0:T(8,128)(2,1)S(1)}, u32[]{:S(2)}, u32[]{:S(2)}) %collective-permute-start.7) | collective-permute-done | bytes 491552 | tf_op jit(solution)/shard_map/ppermute | solution.py:20
  140.7 0.0 copy-done.1
  140.7 0.0 copy-done.2
  140.7 0.0 copy-done.3
  140.7 1.5 inner_step.1
  142.2 0.0 copy-start.6
  142.2 0.0 copy-start.7
  142.2 24.2 %all_to_all.22 = bf16[32,64,128]{2,1,0:T(8,128)(2,1)S(1)} all-to-all(bf16[32,64,128]{2,1,0:T(8,128)(2,1)S(1)} %inner_step.1), channel_id=1, replica_groups=mesh['island'=32,'member'=16] {'island'}, dimensions={0} | all-to-all | bytes 1048576 | tf_op jit(solution)/shard_map/all_to_all | solution.py:260
  166.4 0.1 convert_reduce_fusion
  166.5 0.1 fusion.4
  166.6 0.0 copy-done.6
  166.6 0.0 copy-done.7
  166.6 0.6 fusion.2
  (11 shorter events, 0.2 us)
Async XLA Ops:
  1.4 10.7 %collective-permute-start = (bf16[24,320]{1,0:T(8,128)(2,1)S(1)}, bf16[24,320]{1,0:T(8,128)(2,1)S(1)}, u32[]{:S(2)}, u32[]{:S(2)}) collective-permute-start(bf16[24,320]{1,0:T(8,128)(2,1)S(1)} %bitcast_convert_fusion), channel_id=1, source_target_pairs={{0,2},{1,3},{2,0},{3,1},{4,6},{5,7},{6,4},{7,5},{8,10},{9,11},{10,... | collective-permute-start | bytes 46088 | tf_op jit(solution)/shard_map/ppermute | solution.py:20
  5.7 1.4 copy-start
  7.1 0.7 copy-start.5
  12.2 48.5 %all-to-all-start = ((bf16[8,640,128]{2,1,0:T(8,128)(2,1)}), bf16[8,640,128]{2,1,0:T(8,128)(2,1)S(1)}, u32[]{:S(2)}, u32[]{:S(2)}) async-start(bf16[8,640,128]{2,1,0:T(8,128)(2,1)} %bitcast.4), calls=%async_computation | async-start | bytes 2621440 | tf_op jit(solution)/shard_map/all_to_all | solution.py:24
  21.6 5.8 %collective-permute-start.1 = (bf16[24,640]{1,0:T(8,128)(2,1)S(1)}, bf16[24,640]{1,0:T(8,128)(2,1)S(1)}, u32[]{:S(2)}, u32[]{:S(2)}) collective-permute-start(bf16[24,640]{1,0:T(8,128)(2,1)S(1)} %pad_maximum_fusion), channel_id=1, source_target_pairs={{0,64},{16,80},{32,96},{48,112},{64,0},{80,16},{96,32},{112,48},{1... | collective-permute-start | bytes 92168 | tf_op jit(solution)/shard_map/ppermute | solution.py:230
  27.4 17.7 %collective-permute-start.4 = (bf16[2,24,640]{2,1,0:T(8,128)(2,1)S(1)}, bf16[2,24,640]{2,1,0:T(8,128)(2,1)S(1)}, u32[]{:S(2)}, u32[]{:S(2)}) collective-permute-start(bf16[2,24,640]{2,1,0:T(8,128)(2,1)S(1)} %maximum_select_fusion.1), channel_id=1, source_target_pairs={{0,128},{16,144},{32,160},{48,176},{64,192},{80,208},{96,224},{112... | collective-permute-start | bytes 184328 | tf_op jit(solution)/shard_map/ppermute | solution.py:236
  31.9 13.2 %collective-permute-start.3 = (bf16[2,24,640]{2,1,0:T(8,128)(2,1)S(1)}, bf16[2,24,640]{2,1,0:T(8,128)(2,1)S(1)}, u32[]{:S(2)}, u32[]{:S(2)}) collective-permute-start(bf16[2,24,640]{2,1,0:T(8,128)(2,1)S(1)} %maximum_select_fusion.1), channel_id=1, source_target_pairs={{0,256},{16,272},{32,288},{48,304},{64,320},{80,336},{96,352},{112... | collective-permute-start | bytes 184328 | tf_op jit(solution)/shard_map/ppermute | solution.py:236
  37.0 8.1 %collective-permute-start.2 = (bf16[2,24,640]{2,1,0:T(8,128)(2,1)S(1)}, bf16[2,24,640]{2,1,0:T(8,128)(2,1)S(1)}, u32[]{:S(2)}, u32[]{:S(2)}) collective-permute-start(bf16[2,24,640]{2,1,0:T(8,128)(2,1)S(1)} %maximum_select_fusion.1), channel_id=1, source_target_pairs={{0,384},{16,400},{32,416},{48,432},{64,448},{80,464},{96,480},{112... | collective-permute-start | bytes 184328 | tf_op jit(solution)/shard_map/ppermute | solution.py:236
  62.4 4.2 %collective-permute-start.5 = (bf16[4,768,128]{2,1,0:T(8,128)(2,1)S(1)}, bf16[4,768,128]{2,1,0:T(8,128)(2,1)S(1)}, u32[]{:S(2)}, u32[]{:S(2)}) collective-permute-start(bf16[4,768,128]{2,1,0:T(8,128)(2,1)S(1)} %parts.3), channel_id=1, source_target_pairs={{0,1},{1,0},{2,3},{3,2},{4,5},{5,4},{6,7},{7,6},{8,9},{9,8},{10,11... | collective-permute-start | bytes 2359304 | tf_op jit(solution)/shard_map/ppermute | solution.py:20
  66.1 29.8 %copy-start.4 = (bf16[1,128,768]{2,1,0:T(8,128)(2,1)S(1)}, bf16[1,128,768]{2,1,0:T(8,128)(2,1)}, u32[]{:S(2)}) copy-start(bf16[1,128,768]{2,1,0:T(8,128)(2,1)} %param.9) | copy-start | bytes 589828
  119.6 4.2 %collective-permute-start.6 = (bf16[4,128,768]{2,1,0:T(8,128)(2,1)S(1)}, bf16[4,128,768]{2,1,0:T(8,128)(2,1)S(1)}, u32[]{:S(2)}, u32[]{:S(2)}) collective-permute-start(bf16[4,128,768]{2,1,0:T(8,128)(2,1)S(1)} %all_to_all.21.hm_ref), channel_id=1, source_target_pairs={{0,1},{1,0},{2,3},{3,2},{4,5},{5,4},{6,7},{7,6},{8,9},{9,8},{10,11... | collective-permute-start | bytes 2359304 | tf_op jit(solution)/shard_map/ppermute | solution.py:20
  125.4 15.3 %copy-start.1 = (f32[1,320,768]{2,1,0:T(8,128)S(1)}, f32[1,320,768]{2,1,0:T(8,128)}, u32[]{:S(2)}) copy-start(f32[1,320,768]{2,1,0:T(8,128)} %param.13) | copy-start | bytes 2949124
  125.4 15.3 %copy-start.2 = (f32[1,320,768]{2,1,0:T(8,128)S(1)}, f32[1,320,768]{2,1,0:T(8,128)}, u32[]{:S(2)}) copy-start(f32[1,320,768]{2,1,0:T(8,128)} %param.14) | copy-start | bytes 2949124
  125.4 15.3 %copy-start.3 = (bf16[1,320,768]{2,1,0:T(8,128)(2,1)S(1)}, bf16[1,320,768]{2,1,0:T(8,128)(2,1)}, u32[]{:S(2)}) copy-start(bf16[1,320,768]{2,1,0:T(8,128)(2,1)} %param.15) | copy-start | bytes 1474564
  125.4 15.3 %collective-permute-start.7 = (bf16[320,768]{1,0:T(8,128)(2,1)S(1)}, bf16[320,768]{1,0:T(8,128)(2,1)S(1)}, u32[]{:S(2)}, u32[]{:S(2)}) collective-permute-start(bf16[320,768]{1,0:T(8,128)(2,1)S(1)} %team_grad.3), channel_id=1, source_target_pairs={{0,2},{1,3},{2,0},{3,1},{4,6},{5,7},{6,4},{7,5},{8,10},{9,11},{10,... | collective-permute-start | bytes 1474568 | tf_op jit(solution)/shard_map/ppermute | solution.py:20
  142.2 24.4 %copy-start.6 = (f32[320,24]{0,1:T(8,128)S(1)}, f32[320,24]{0,1:T(8,128)}, u32[]{:S(2)}) copy-start(f32[320,24]{0,1:T(8,128)} %param.11) | copy-start | bytes 92164
  142.2 24.4 %copy-start.7 = (f32[320,24]{0,1:T(8,128)S(1)}, f32[320,24]{0,1:T(8,128)}, u32[]{:S(2)}) copy-start(f32[320,24]{0,1:T(8,128)} %param.12) | copy-start | bytes 92164

commit v4 on v3

--- a/solution.py
+++ b/solution.py
@@ -16,8 +16,14 @@
 PACKED = 64
 
 
-def swap(x, bit):
-    return lax.ppermute(x, "member", [(m, m ^ bit) for m in range(MEMBERS)])
+def swap(x):
+    return lax.ppermute(x, "member", [(m, m ^ 1) for m in range(MEMBERS)])
+
+
+def to_neighbour(x, by):
+    return lax.ppermute(
+        x, "member", [(m, (m + 2 * (by if m % 2 == 0 else -by)) % MEMBERS) for m in range(MEMBERS)]
+    )
 
 
 def exchange(x, groups):
@@ -27,12 +33,24 @@
 
 
 def pick_kernel(q_ref, tok_ref, slot_ref, out_ref):
+    step = pl.program_id(0)
     shape = (tok_ref.shape[0], slot_ref.shape[1])
     chosen = (lax.broadcasted_iota(jnp.int32, shape, 0) == slot_ref[...]).astype(BF)
     got = lax.dot_general(
         tok_ref[...], chosen, (((0,), (0,)), ((), ())), preferred_element_type=F32
-    )
-    out_ref[...] = got.astype(BF).reshape(out_ref.shape)
+    ).astype(BF)
+    rows = got.shape[0] // 2
+    chip = 2 * (step & 3) + ((step >> 2) ^ q_ref[0])
+
+    @pl.when(step < NA)
+    def _():
+        for c in range(2):
+            out_ref[step, c, 0:rows] = got[c * rows : (c + 1) * rows]
+
+    @pl.when(step >= NA)
+    def _():
+        out_ref[((chip + 1) >> 1) & 3, 0, rows : 2 * rows] = got[:rows]
+        out_ref[((chip + 7) >> 1) & 3, 1, rows : 2 * rows] = got[rows:]
 
 
 def pick(q, tokens, slot_token, rows):
@@ -41,17 +59,17 @@
         pick_kernel,
         grid_spec=pltpu.PrefetchScalarGridSpec(
             num_scalar_prefetch=1,
-            grid=(NA, 2),
+            grid=(2 * NA,),
             in_specs=[
                 pl.BlockSpec(
                     (tokens.shape[0], 2 * rows),
-                    lambda i, j, q: (0, 2 * i + q[0] + j - 2 * q[0] * j),
+                    lambda i, q: (0, 2 * (i & 3) + ((i >> 2) ^ q[0])),
                 ),
-                pl.BlockSpec((1, slots), lambda i, j, q: (0, 0)),
+                pl.BlockSpec((1, slots), lambda i, q: (0, 0)),
             ],
-            out_specs=pl.BlockSpec((1, 2, 1, rows, slots), lambda i, j, q: (i, 0, j, 0, 0)),
-        ),
-        out_shape=jax.ShapeDtypeStruct((NA, 2, 2, rows, slots), BF),
+            out_specs=pl.BlockSpec((NA, 2, 2 * rows, slots), lambda i, q: (0, 0, 0, 0)),
+        ),
+        out_shape=jax.ShapeDtypeStruct((NA, 2, 2 * rows, slots), BF),
         compiler_params=pltpu.CompilerParams(vmem_limit_bytes=VMEM),
         name="pick",
     )(q, tokens, slot_token).reshape(2 * NA, 2 * rows, slots)
@@ -225,7 +243,7 @@
     picked = pick(q.reshape(1), tokens[0], slot_token, rows)
 
     low = weight_t.astype(BF)
-    low = jnp.concatenate([low, swap(low, 2)], axis=1)
+    low = jnp.concatenate([low, to_neighbour(low, 1)], axis=1)
     picked, low = lax.optimization_barrier((picked, low))
     near = lax.ppermute(low, "island", [(i, i ^ NX) for i in range(NX * NY)])
     routed = exchange(picked, TEAM).reshape(NA, 2, 2 * rows, slots)
@@ -246,15 +264,15 @@
         column.reshape(NY * cols, 2 * rows), "island", axis=0, tiled=True, axis_index_groups=ALONG_X
     )
 
-    sent = swap(parts(other, routed, weights), 1)
+    sent = swap(parts(other, routed, weights))
     kept = parts(mine, routed, weights)
     summed = (kept.astype(F32) + sent.astype(F32)).astype(BF)
     hid = hidden(exchange(summed, SAME_CORE), cotangent[0], scale)
     hid_mine = exchange(hid, SAME_CORE)
-    hid_other = swap(hid_mine, 1)
+    hid_other = swap(hid_mine)
 
     routed = routed.reshape(NA, 2, 2, rows, slots)
-    far = swap(team_grad(mine, 1, routed, hid_mine, hid_other, BF), 2)
+    far = to_neighbour(team_grad(mine, 1, routed, hid_mine, hid_other, BF), -1)
     own = team_grad(mine, 0, routed, hid_mine, hid_other, F32)
     moved = inner_step(own, far, first_moment[0], second_moment[0], error_state[0], scale, cols)
     shares = lax.all_to_all(

time: 168 us -> 164 us (0.976)
  waiting for transfers between devices: 20.6 us -> 16.1 us
    ppermute x4, waiting for transfers between devices: 14.3 us -> 9.81 us  [the longest x2 7.09 us: to_neighbour(): lax.ppermute(x, 'member', [(m, (m + 2 * (by if m % 2 == 0 else -by)) % ME...]
    ppermute x4, starting transfers between devices: 10.2 us -> 13.7 us  [the longest x2 9.88 us: to_neighbour(): lax.ppermute(x, 'member', [(m, (m + 2 * (by if m % 2 == 0 else -by)) % ME...]
    all_to_all x1, starting transfers between devices: 9.4 us -> 7.03 us  [exchange(): lax.all_to_all(x, 'member', split_axis=0, concat_axis=0, tiled=True, axis...]
  transfers between devices with their start and end apart: 9 -> 9, of which waited for: 5 -> 6; matrix products, arithmetic and copies ran while one was open for 0% -> 0% of each run, Pallas kernels for 5% -> 5%
where the time goes in v4:
time: 164 us; the launch traced here: 163 us
  blocking collectives  91.6 us (56%)
  starting transfers between devices  37.9 us (23%)
  waiting for transfers between devices  16.1 us (10%)
  Pallas kernels  12.4 us (8%)
  local copies, waits for them, and re-layouts  2.25 us (1%)
  other arithmetic  1.85 us (1%)
    all_to_all x2, blocking collectives, exchange(): lax.all_to_all(x, 'member', split_axis=0, concat_axis=0, tiled=True, axis...  51.3 us
    all_to_all x1, blocking collectives, local(): lax.all_to_all(moved, 'island', split_axis=0, concat_axis=0, tiled=True)  24.9 us
    all_gather x1, blocking collectives, local(): lax.all_gather(column.reshape(NY * cols, 2 * rows), 'island', axis=0, til...  15.4 us
    ppermute x3, starting transfers between devices, local(): lax.ppermute(pair, 'island', [(i, (i + 2 * NX * k) % (NX * NY)) for i in...  14.8 us
    ppermute x2, starting transfers between devices, to_neighbour(): lax.ppermute(x, 'member', [(m, (m + 2 * (by if m % 2 == 0 else -by)) % ME...  9.88 us
    ppermute x2, waiting for transfers between devices, to_neighbour(): lax.ppermute(x, 'member', [(m, (m + 2 * (by if m % 2 == 0 else -by)) % ME...  7.09 us
    all_to_all x1, starting transfers between devices, exchange(): lax.all_to_all(x, 'member', split_axis=0, concat_axis=0, tiled=True, axis...  7.03 us
    pallas_call x1, Pallas kernels, pick(): pl.pallas_call(pick_kernel, grid_spec=pltpu.PrefetchScalarGridSpec(num_sc...  3.98 us
  transfers between devices with their start and end apart: 9, of which 6 were waited for; matrix products, arithmetic and copies ran while one was open for 0% of the time, Pallas kernels for 5%

profile of v4, /device:TPU:8, one launch (start us, length us, event | category | flops | bytes accessed | tf_op | source)
XLA Modules:
  0.0 162.9 jit_solution(5607230061365545228)
XLA Ops:
  0.6 0.8 bitcast_convert_fusion
  1.4 4.3 %collective-permute-start = (bf16[24,320]{1,0:T(8,128)(2,1)S(1)}, bf16[24,320]{1,0:T(8,128)(2,1)S(1)}, u32[]{:S(2)}, u32[]{:S(2)}) collective-permute-start(bf16[24,320]{1,0:T(8,128)(2,1)S(1)} %bitcast_convert_fusion), channel_id=1, source_target_pairs={{0,2},{1,15},{2,4},{3,1},{4,6},{5,3},{6,8},{7,5},{8,10},{9,7},{10,... | collective-permute-start | bytes 46088 | tf_op jit(solution)/shard_map/ppermute | solution.py:24
  5.7 0.0 copy-start
  5.7 1.4 copy-done
  7.1 0.0 copy-start.5
  7.1 0.7 copy-done.5
  7.7 4.0 %pick.1 = bf16[4,2,640,128]{3,2,1,0:T(8,128)(2,1)} custom-call(s32[1]{0:T(128)} %bitcast.2.q_ref, bf16[144,5120]{1,0:T(8,128)(2,1)S(1)} %bitcast.52, s32[1,128]{1,0:T(1,128)S(1)} %copy-done.5), custom_call_target="tpu_custom_call" | custom-call | tf_op jit(solution)/shard_map/pick/pallas_call | solution.py:58
  11.7 2.4 %collective-permute-done = bf16[24,320]{1,0:T(8,128)(2,1)S(1)} collective-permute-done((bf16[24,320]{1,0:T(8,128)(2,1)S(1)}, bf16[24,320]{1,0:T(8,128)(2,1)S(1)}, u32[]{:S(2)}, u32[]{:S(2)}) %collective-permute-start) | collective-permute-done | bytes 15392 | tf_op jit(solution)/shard_map/ppermute | solution.py:24
  14.1 0.1 pad_maximum_fusion
  14.1 7.0 %all-to-all-start = ((bf16[8,640,128]{2,1,0:T(8,128)(2,1)}), bf16[8,640,128]{2,1,0:T(8,128)(2,1)S(1)}, u32[]{:S(2)}, u32[]{:S(2)}) async-start(bf16[8,640,128]{2,1,0:T(8,128)(2,1)} %bitcast.4), calls=%async_computation | async-start | bytes 2621440 | tf_op jit(solution)/shard_map/all_to_all | solution.py:30
  21.2 2.3 %collective-permute-start.1 = (bf16[24,640]{1,0:T(8,128)(2,1)S(1)}, bf16[24,640]{1,0:T(8,128)(2,1)S(1)}, u32[]{:S(2)}, u32[]{:S(2)}) collective-permute-start(bf16[24,640]{1,0:T(8,128)(2,1)S(1)} %pad_maximum_fusion), channel_id=1, source_target_pairs={{0,64},{16,80},{32,96},{48,112},{64,0},{80,16},{96,32},{112,48},{1... | collective-permute-start | bytes 92168 | tf_op jit(solution)/shard_map/ppermute | solution.py:248
  23.5 3.4 %collective-permute-done.1 = bf16[24,640]{1,0:T(8,128)(2,1)S(1)} collective-permute-done((bf16[24,640]{1,0:T(8,128)(2,1)S(1)}, bf16[24,640]{1,0:T(8,128)(2,1)S(1)}, u32[]{:S(2)}, u32[]{:S(2)}) %collective-permute-start.1) | collective-permute-done | bytes 30752 | tf_op jit(solution)/shard_map/ppermute | solution.py:248
  27.0 4.5 %collective-permute-start.4 = (bf16[2,24,640]{2,1,0:T(8,128)(2,1)S(1)}, bf16[2,24,640]{2,1,0:T(8,128)(2,1)S(1)}, u32[]{:S(2)}, u32[]{:S(2)}) collective-permute-start(bf16[2,24,640]{2,1,0:T(8,128)(2,1)S(1)} %maximum_select_fusion.1), channel_id=1, source_target_pairs={{0,128},{16,144},{32,160},{48,176},{64,192},{80,208},{96,224},{112... | collective-permute-start | bytes 184328 | tf_op jit(solution)/shard_map/ppermute | solution.py:254
  31.5 5.0 %collective-permute-start.3 = (bf16[2,24,640]{2,1,0:T(8,128)(2,1)S(1)}, bf16[2,24,640]{2,1,0:T(8,128)(2,1)S(1)}, u32[]{:S(2)}, u32[]{:S(2)}) collective-permute-start(bf16[2,24,640]{2,1,0:T(8,128)(2,1)S(1)} %maximum_select_fusion.1), channel_id=1, source_target_pairs={{0,256},{16,272},{32,288},{48,304},{64,320},{80,336},{96,352},{112... | collective-permute-start | bytes 184328 | tf_op jit(solution)/shard_map/ppermute | solution.py:254
  36.5 5.2 %collective-permute-start.2 = (bf16[2,24,640]{2,1,0:T(8,128)(2,1)S(1)}, bf16[2,24,640]{2,1,0:T(8,128)(2,1)S(1)}, u32[]{:S(2)}, u32[]{:S(2)}) collective-permute-start(bf16[2,24,640]{2,1,0:T(8,128)(2,1)S(1)} %maximum_select_fusion.1), channel_id=1, source_target_pairs={{0,384},{16,400},{32,416},{48,432},{64,448},{80,464},{96,480},{112... | collective-permute-start | bytes 184328 | tf_op jit(solution)/shard_map/ppermute | solution.py:254
  41.8 2.9 %collective-permute-done.2 = bf16[2,24,640]{2,1,0:T(8,128)(2,1)S(1)} collective-permute-done((bf16[2,24,640]{2,1,0:T(8,128)(2,1)S(1)}, bf16[2,24,640]{2,1,0:T(8,128)(2,1)S(1)}, u32[]{:S(2)}, u32[]{:S(2)}) %collective-permute-start.2) | collective-permute-done | bytes 61472 | tf_op jit(solution)/shard_map/ppermute | solution.py:254
  44.7 0.0 collective-permute-done.3
  44.7 0.0 collective-permute-done.4
  44.9 15.4 %all_gather.3.w_ref = bf16[768,640]{1,0:T(8,128)(2,1)S(1)} all-gather(bf16[192,640]{1,0:T(8,128)(2,1)S(1)} %bitcast.57), channel_id=1, replica_groups={{0,16,32,48},{64,80,96,112},{128,144,160,176},{192,208,224,240},{256,27..., dimensions={0}, use_global_device_ids=true | all-gather | bytes 1228800 | tf_op jit(solution)/shard_map/all_gather | solution.py:263
  60.3 0.0 all-to-all-done
  60.3 1.7 %parts.3 = bf16[4,768,128]{2,1,0:T(8,128)(2,1)S(1)} custom-call(s32[1]{0:T(128)S(6)} %sub.10.which_ref, bf16[4,2,640,128]{3,2,1,0:T(8,128)(2,1)S(1)} %bitcast.46, bf16[768,640]{1,0:T(8,128)(2,1)S(1)} %all_gather.3.w_ref), custom_call_target="tpu_custom_call" | custom-call | flops 503316480 | bytes 2424832 | tf_op jit(solution)/shard_map/parts/pallas_call | solution.py:85
  62.0 1.9 %collective-permute-start.5 = (bf16[4,768,128]{2,1,0:T(8,128)(2,1)S(1)}, bf16[4,768,128]{2,1,0:T(8,128)(2,1)S(1)}, u32[]{:S(2)}, u32[]{:S(2)}) collective-permute-start(bf16[4,768,128]{2,1,0:T(8,128)(2,1)S(1)} %parts.3), channel_id=1, source_target_pairs={{0,1},{1,0},{2,3},{3,2},{4,5},{5,4},{6,7},{7,6},{8,9},{9,8},{10,11... | collective-permute-start | bytes 2359304 | tf_op jit(solution)/shard_map/ppermute | solution.py:20
  64.0 1.8 %parts.2 = bf16[4,768,128]{2,1,0:T(8,128)(2,1)S(1)} custom-call(s32[1]{0:T(128)} %bitcast.1.which_ref, bf16[4,2,640,128]{3,2,1,0:T(8,128)(2,1)S(1)} %bitcast.47, bf16[768,640]{1,0:T(8,128)(2,1)S(1)} %all_gather.3.w_ref), custom_call_target="tpu_custom_call" | custom-call | flops 503316480 | bytes 2424832 | tf_op jit(solution)/shard_map/parts/pallas_call | solution.py:85
  65.7 0.0 copy-start.4
  65.7 0.5 collective-permute-done.5
  66.2 0.2 add_convert_fusion
  66.4 28.9 %all_to_all.20.refs_0_ = bf16[4,768,128]{2,1,0:T(8,128)(2,1)S(1)} all-to-all(bf16[4,768,128]{2,1,0:T(8,128)(2,1)S(1)} %add_convert_fusion), channel_id=1, replica_groups={{0,4,8,12},{1,5,9,13},{2,6,10,14},{3,7,11,15},{16,20,24,28},{17,21,25,2..., dimensions={0} | all-to-all | bytes 1572864 | tf_op jit(solution)/shard_map/all_to_all | solution.py:30
  95.3 0.0 copy-done.4
  95.3 0.3 hidden.1
  95.6 22.4 %all_to_all.21.hm_ref = bf16[4,128,768]{2,1,0:T(8,128)(2,1)S(1)} all-to-all(bf16[4,128,768]{2,1,0:T(8,128)(2,1)S(1)} %hidden.1), channel_id=1, replica_groups={{0,4,8,12},{1,5,9,13},{2,6,10,14},{3,7,11,15},{16,20,24,28},{17,21,25,2..., dimensions={0} | all-to-all | bytes 1572864 | tf_op jit(solution)/shard_map/all_to_all | solution.py:30
  118.0 1.9 %collective-permute-start.6 = (bf16[4,128,768]{2,1,0:T(8,128)(2,1)S(1)}, bf16[4,128,768]{2,1,0:T(8,128)(2,1)S(1)}, u32[]{:S(2)}, u32[]{:S(2)}) collective-permute-start(bf16[4,128,768]{2,1,0:T(8,128)(2,1)S(1)} %all_to_all.21.hm_ref), channel_id=1, source_target_pairs={{0,1},{1,0},{2,3},{3,2},{4,5},{5,4},{6,7},{7,6},{8,9},{9,8},{10,11... | collective-permute-start | bytes 2359304 | tf_op jit(solution)/shard_map/ppermute | solution.py:20
  119.9 2.3 %collective-permute-done.6.ho_ref = bf16[4,128,768]{2,1,0:T(8,128)(2,1)S(1)} collective-permute-done((bf16[4,128,768]{2,1,0:T(8,128)(2,1)S(1)}, bf16[4,128,768]{2,1,0:T(8,128)(2,1)S(1)}, u32[]{:S(2)}, u32[]{:S(2)}) %collective-permute-start.6) | collective-permute-done | bytes 786464 | tf_op jit(solution)/shard_map/ppermute | solution.py:20
  122.1 1.6 team_grad.3
  123.7 0.0 copy-start.1
  123.7 0.0 copy-start.2
  123.7 0.0 copy-start.3
  123.7 5.6 %collective-permute-start.7 = (bf16[320,768]{1,0:T(8,128)(2,1)S(1)}, bf16[320,768]{1,0:T(8,128)(2,1)S(1)}, u32[]{:S(2)}, u32[]{:S(2)}) collective-permute-start(bf16[320,768]{1,0:T(8,128)(2,1)S(1)} %team_grad.3), channel_id=1, source_target_pairs={{0,14},{1,3},{2,0},{3,5},{4,2},{5,7},{6,4},{7,9},{8,6},{9,11},{10,... | collective-permute-start | bytes 1474568 | tf_op jit(solution)/shard_map/ppermute | solution.py:24
  129.4 1.6 team_grad.2.refs_0_
  131.0 4.7 %collective-permute-done.7.refs_1_ = bf16[320,768]{1,0:T(8,128)(2,1)S(1)} collective-permute-done((bf16[320,768]{1,0:T(8,128)(2,1)S(1)}, bf16[320,768]{1,0:T(8,128)(2,1)S(1)}, u32[]{:S(2)}, u32[]{:S(2)}) %collective-permute-start.7) | collective-permute-done | bytes 491552 | tf_op jit(solution)/shard_map/ppermute | solution.py:24
  135.7 0.0 copy-done.1
  135.7 0.0 copy-done.2
  135.7 0.0 copy-done.3
  135.7 1.4 inner_step.1
  137.1 0.0 copy-start.6
  137.2 0.0 copy-start.7
  137.2 24.9 %all_to_all.22 = bf16[32,64,128]{2,1,0:T(8,128)(2,1)S(1)} all-to-all(bf16[32,64,128]{2,1,0:T(8,128)(2,1)S(1)} %inner_step.1), channel_id=1, replica_groups=mesh['island'=32,'member'=16] {'island'}, dimensions={0} | all-to-all | bytes 1048576 | tf_op jit(solution)/shard_map/all_to_all | solution.py:278
  162.1 0.1 convert_reduce_fusion
  162.2 0.1 fusion.4
  162.2 0.0 copy-done.6
  162.2 0.0 copy-done.7
  162.2 0.6 fusion.2
  (11 shorter events, 0.2 us)
Async XLA Ops:
  1.4 12.7 %collective-permute-start = (bf16[24,320]{1,0:T(8,128)(2,1)S(1)}, bf16[24,320]{1,0:T(8,128)(2,1)S(1)}, u32[]{:S(2)}, u32[]{:S(2)}) collective-permute-start(bf16[24,320]{1,0:T(8,128)(2,1)S(1)} %bitcast_convert_fusion), channel_id=1, source_target_pairs={{0,2},{1,15},{2,4},{3,1},{4,6},{5,3},{6,8},{7,5},{8,10},{9,7},{10,... | collective-permute-start | bytes 46088 | tf_op jit(solution)/shard_map/ppermute | solution.py:24
  5.7 1.4 copy-start
  7.1 0.7 copy-start.5
  14.1 46.1 %all-to-all-start = ((bf16[8,640,128]{2,1,0:T(8,128)(2,1)}), bf16[8,640,128]{2,1,0:T(8,128)(2,1)S(1)}, u32[]{:S(2)}, u32[]{:S(2)}) async-start(bf16[8,640,128]{2,1,0:T(8,128)(2,1)} %bitcast.4), calls=%async_computation | async-start | bytes 2621440 | tf_op jit(solution)/shard_map/all_to_all | solution.py:30
  21.2 5.8 %collective-permute-start.1 = (bf16[24,640]{1,0:T(8,128)(2,1)S(1)}, bf16[24,640]{1,0:T(8,128)(2,1)S(1)}, u32[]{:S(2)}, u32[]{:S(2)}) collective-permute-start(bf16[24,640]{1,0:T(8,128)(2,1)S(1)} %pad_maximum_fusion), channel_id=1, source_target_pairs={{0,64},{16,80},{32,96},{48,112},{64,0},{80,16},{96,32},{112,48},{1... | collective-permute-start | bytes 92168 | tf_op jit(solution)/shard_map/ppermute | solution.py:248
  27.0 17.8 %collective-permute-start.4 = (bf16[2,24,640]{2,1,0:T(8,128)(2,1)S(1)}, bf16[2,24,640]{2,1,0:T(8,128)(2,1)S(1)}, u32[]{:S(2)}, u32[]{:S(2)}) collective-permute-start(bf16[2,24,640]{2,1,0:T(8,128)(2,1)S(1)} %maximum_select_fusion.1), channel_id=1, source_target_pairs={{0,128},{16,144},{32,160},{48,176},{64,192},{80,208},{96,224},{112... | collective-permute-start | bytes 184328 | tf_op jit(solution)/shard_map/ppermute | solution.py:254
  31.5 13.2 %collective-permute-start.3 = (bf16[2,24,640]{2,1,0:T(8,128)(2,1)S(1)}, bf16[2,24,640]{2,1,0:T(8,128)(2,1)S(1)}, u32[]{:S(2)}, u32[]{:S(2)}) collective-permute-start(bf16[2,24,640]{2,1,0:T(8,128)(2,1)S(1)} %maximum_select_fusion.1), channel_id=1, source_target_pairs={{0,256},{16,272},{32,288},{48,304},{64,320},{80,336},{96,352},{112... | collective-permute-start | bytes 184328 | tf_op jit(solution)/shard_map/ppermute | solution.py:254
  36.5 8.2 %collective-permute-start.2 = (bf16[2,24,640]{2,1,0:T(8,128)(2,1)S(1)}, bf16[2,24,640]{2,1,0:T(8,128)(2,1)S(1)}, u32[]{:S(2)}, u32[]{:S(2)}) collective-permute-start(bf16[2,24,640]{2,1,0:T(8,128)(2,1)S(1)} %maximum_select_fusion.1), channel_id=1, source_target_pairs={{0,384},{16,400},{32,416},{48,432},{64,448},{80,464},{96,480},{112... | collective-permute-start | bytes 184328 | tf_op jit(solution)/shard_map/ppermute | solution.py:254
  62.0 4.2 %collective-permute-start.5 = (bf16[4,768,128]{2,1,0:T(8,128)(2,1)S(1)}, bf16[4,768,128]{2,1,0:T(8,128)(2,1)S(1)}, u32[]{:S(2)}, u32[]{:S(2)}) collective-permute-start(bf16[4,768,128]{2,1,0:T(8,128)(2,1)S(1)} %parts.3), channel_id=1, source_target_pairs={{0,1},{1,0},{2,3},{3,2},{4,5},{5,4},{6,7},{7,6},{8,9},{9,8},{10,11... | collective-permute-start | bytes 2359304 | tf_op jit(solution)/shard_map/ppermute | solution.py:20
  65.7 29.6 %copy-start.4 = (bf16[1,128,768]{2,1,0:T(8,128)(2,1)S(1)}, bf16[1,128,768]{2,1,0:T(8,128)(2,1)}, u32[]{:S(2)}) copy-start(bf16[1,128,768]{2,1,0:T(8,128)(2,1)} %param.9) | copy-start | bytes 589828
  118.0 4.2 %collective-permute-start.6 = (bf16[4,128,768]{2,1,0:T(8,128)(2,1)S(1)}, bf16[4,128,768]{2,1,0:T(8,128)(2,1)S(1)}, u32[]{:S(2)}, u32[]{:S(2)}) collective-permute-start(bf16[4,128,768]{2,1,0:T(8,128)(2,1)S(1)} %all_to_all.21.hm_ref), channel_id=1, source_target_pairs={{0,1},{1,0},{2,3},{3,2},{4,5},{5,4},{6,7},{7,6},{8,9},{9,8},{10,11... | collective-permute-start | bytes 2359304 | tf_op jit(solution)/shard_map/ppermute | solution.py:20
  123.7 12.0 %copy-start.1 = (f32[1,320,768]{2,1,0:T(8,128)S(1)}, f32[1,320,768]{2,1,0:T(8,128)}, u32[]{:S(2)}) copy-start(f32[1,320,768]{2,1,0:T(8,128)} %param.13) | copy-start | bytes 2949124
  123.7 12.0 %copy-start.2 = (f32[1,320,768]{2,1,0:T(8,128)S(1)}, f32[1,320,768]{2,1,0:T(8,128)}, u32[]{:S(2)}) copy-start(f32[1,320,768]{2,1,0:T(8,128)} %param.14) | copy-start | bytes 2949124
  123.7 12.0 %copy-start.3 = (bf16[1,320,768]{2,1,0:T(8,128)(2,1)S(1)}, bf16[1,320,768]{2,1,0:T(8,128)(2,1)}, u32[]{:S(2)}) copy-start(bf16[1,320,768]{2,1,0:T(8,128)(2,1)} %param.15) | copy-start | bytes 1474564
  123.7 11.9 %collective-permute-start.7 = (bf16[320,768]{1,0:T(8,128)(2,1)S(1)}, bf16[320,768]{1,0:T(8,128)(2,1)S(1)}, u32[]{:S(2)}, u32[]{:S(2)}) collective-permute-start(bf16[320,768]{1,0:T(8,128)(2,1)S(1)} %team_grad.3), channel_id=1, source_target_pairs={{0,14},{1,3},{2,0},{3,5},{4,2},{5,7},{6,4},{7,9},{8,6},{9,11},{10,... | collective-permute-start | bytes 1474568 | tf_op jit(solution)/shard_map/ppermute | solution.py:24
  137.1 25.1 %copy-start.6 = (f32[320,24]{0,1:T(8,128)S(1)}, f32[320,24]{0,1:T(8,128)}, u32[]{:S(2)}) copy-start(f32[320,24]{0,1:T(8,128)} %param.11) | copy-start | bytes 92164
  137.2 25.1 %copy-start.7 = (f32[320,24]{0,1:T(8,128)S(1)}, f32[320,24]{0,1:T(8,128)}, u32[]{:S(2)}) copy-start(f32[320,24]{0,1:T(8,128)} %param.12) | copy-start | bytes 92164

commit v5 on v4

--- a/solution.py
+++ b/solution.py
@@ -7,6 +7,7 @@
 
 NY, NX, NA = 8, 4, 4
 ALONG_X = [[y * NX + x for x in range(NX)] for y in range(NY)]
+PAIRS = [[(2 * p + b) * NX + x for p in range(NY // 2)] for b in range(2) for x in range(NX)]
 TEAM = [[4 * a + 2 * q + c for a in range(NA) for c in range(2)] for q in range(2)]
 SAME_CORE = [[4 * a + 2 * q + c for a in range(NA)] for q in range(2) for c in range(2)]
 MEMBERS = 4 * NA
@@ -14,6 +15,7 @@
 F32 = jnp.float32
 VMEM = 16 * 2**20
 PACKED = 64
+WHOLE = pl.BlockSpec(memory_space=pltpu.VMEM)
 
 
 def swap(x):
@@ -76,7 +78,10 @@
 
 
 def parts_kernel(which_ref, x_ref, w_ref, out_ref):
-    out_ref[0] = jnp.dot(w_ref[...], x_ref[0, 0], preferred_element_type=F32).astype(BF)
+    for a in range(x_ref.shape[0]):
+        out_ref[a] = jnp.dot(
+            w_ref[...], x_ref[a, which_ref[0]], preferred_element_type=F32
+        ).astype(BF)
 
 
 def parts(which, routed, weights):
@@ -84,15 +89,8 @@
     ff = weights.shape[0]
     return pl.pallas_call(
         parts_kernel,
-        grid_spec=pltpu.PrefetchScalarGridSpec(
-            num_scalar_prefetch=1,
-            grid=(na,),
-            in_specs=[
-                pl.BlockSpec((1, 1, depth, slots), lambda i, which: (i, which[0], 0, 0)),
-                pl.BlockSpec((ff, depth), lambda i, which: (0, 0)),
-            ],
-            out_specs=pl.BlockSpec((1, ff, slots), lambda i, which: (i, 0, 0)),
-        ),
+        in_specs=[pl.BlockSpec(memory_space=pltpu.SMEM)] + [WHOLE] * 2,
+        out_specs=WHOLE,
         out_shape=jax.ShapeDtypeStruct((na, ff, slots), BF),
         compiler_params=pltpu.CompilerParams(vmem_limit_bytes=VMEM),
         cost_estimate=pl.CostEstimate(
@@ -123,50 +121,36 @@
     na, ff, slots = partial.shape
     return pl.pallas_call(
         lambda *refs: hidden_kernel(scale, *refs),
-        in_specs=[pl.BlockSpec(memory_space=pltpu.VMEM)] * 2,
-        out_specs=pl.BlockSpec(memory_space=pltpu.VMEM),
+        in_specs=[WHOLE] * 2,
+        out_specs=WHOLE,
         out_shape=jax.ShapeDtypeStruct((na, slots, ff), BF),
         compiler_params=pltpu.CompilerParams(vmem_limit_bytes=VMEM),
         name="hidden",
     )(partial, cot)
 
 
-def grad_kernel(which_ref, xm_ref, xo_ref, hm_ref, ho_ref, out_ref, acc_ref):
-    step = pl.program_id(0)
-    left = jnp.concatenate([xm_ref[0, 0, 0], xo_ref[0, 0, 0]], axis=1)
-    right = jnp.concatenate([hm_ref[0], ho_ref[0]], axis=0)
-    part = jnp.dot(left, right, preferred_element_type=F32)
-
-    @pl.when(step == 0)
-    def _():
-        acc_ref[...] = part
-
-    @pl.when(step > 0)
-    def _():
-        acc_ref[...] += part
-
-    @pl.when(step == pl.num_programs(0) - 1)
-    def _():
-        out_ref[...] = acc_ref[...].astype(out_ref.dtype)
+def grad_kernel(block, which_ref, x_ref, hm_ref, ho_ref, out_ref):
+    core = which_ref[0]
+    na = x_ref.shape[0]
+    left = jnp.concatenate(
+        [x_ref[a, c, block] for a in range(na) for c in (core, 1 - core)], axis=1
+    )
+    for k in range(0, out_ref.shape[1], 256):
+        right = jnp.concatenate(
+            [h[a, :, k : k + 256] for a in range(na) for h in (hm_ref, ho_ref)], axis=0
+        )
+        out_ref[:, k : k + 256] = jnp.dot(left, right, preferred_element_type=F32).astype(
+            out_ref.dtype
+        )
 
 
 def team_grad(which, block, routed, hid_mine, hid_other, dtype):
     na, _, _, rows, slots = routed.shape
     ff = hid_mine.shape[2]
     return pl.pallas_call(
-        grad_kernel,
-        grid_spec=pltpu.PrefetchScalarGridSpec(
-            num_scalar_prefetch=1,
-            grid=(na,),
-            in_specs=[
-                pl.BlockSpec((1, 1, 1, rows, slots), lambda i, w: (i, w[0], block, 0, 0)),
-                pl.BlockSpec((1, 1, 1, rows, slots), lambda i, w: (i, 1 - w[0], block, 0, 0)),
-                pl.BlockSpec((1, slots, ff), lambda i, w: (i, 0, 0)),
-                pl.BlockSpec((1, slots, ff), lambda i, w: (i, 0, 0)),
-            ],
-            out_specs=pl.BlockSpec((rows, ff), lambda i, w: (0, 0)),
-            scratch_shapes=[pltpu.VMEM((rows, ff), F32)],
-        ),
+        lambda *refs: grad_kernel(block, *refs),
+        in_specs=[pl.BlockSpec(memory_space=pltpu.SMEM)] + [WHOLE] * 3,
+        out_specs=WHOLE,
         out_shape=jax.ShapeDtypeStruct((rows, ff), dtype),
         compiler_params=pltpu.CompilerParams(vmem_limit_bytes=VMEM),
         cost_estimate=pl.CostEstimate(
@@ -175,7 +159,7 @@
             transcendentals=0,
         ),
         name="team_grad",
-    )(which, routed, routed, hid_mine, hid_other)
+    )(which, routed, hid_mine, hid_other)
 
 
 def pack(x):
@@ -198,22 +182,23 @@
 
 
 def step_kernel(scale, cols, own_ref, far_ref, m1_ref, m2_ref, err_ref, out_ref):
-    grad = (own_ref[...] + far_ref[...].astype(F32)) * scale
-    one = 0.9 * m1_ref[...] + 0.1 * grad
-    two = 0.95 * m2_ref[...] + 0.05 * grad * grad
-    moved = 0.25 * (one / (jnp.sqrt(two) + 1e-08)) + err_ref[...].astype(F32)
-    out_ref[...] = pack(moved.T.reshape(-1, cols, moved.shape[0])).astype(BF)
+    rows, ff = own_ref.shape
+    wide = 16 * cols
+    for k in range(0, ff, wide):
+        at = slice(k, k + wide)
+        grad = (own_ref[:, at] + far_ref[:, at].astype(F32)) * scale
+        one = 0.9 * m1_ref[:, at] + 0.1 * grad
+        two = 0.95 * m2_ref[:, at] + 0.05 * grad * grad
+        moved = 0.25 * (one / (jnp.sqrt(two) + 1e-08)) + err_ref[:, at].astype(F32)
+        out_ref[k // cols : (k + wide) // cols] = pack(moved.T.reshape(-1, cols, rows)).astype(BF)
 
 
 def inner_step(own, far, m1, m2, err, scale, cols):
-    rows, ff = own.shape
-    blk = ff // 2
-    spec = pl.BlockSpec((rows, blk), lambda i: (0, i))
+    ff = own.shape[1]
     return pl.pallas_call(
         lambda *refs: step_kernel(scale, cols, *refs),
-        grid=(ff // blk,),
-        in_specs=[spec] * 5,
-        out_specs=pl.BlockSpec((blk // cols, PACKED, 128), lambda i: (i, 0, 0)),
+        in_specs=[WHOLE] * 5,
+        out_specs=WHOLE,
         out_shape=jax.ShapeDtypeStruct((ff // cols, PACKED, 128), BF),
         compiler_params=pltpu.CompilerParams(vmem_limit_bytes=VMEM),
         name="inner_step",
@@ -250,18 +235,11 @@
     y = lax.axis_index("island") >> 2
     odd = (y & 1) == 1
     pair = jnp.where(odd, jnp.stack([near, low]), jnp.stack([low, near]))
-    ring = [pair] + [
-        lax.ppermute(
-            pair,
-            "island",
-            [(i, (i + 2 * NX * k) % (NX * NY)) for i in range(NX * NY)],
-        )
-        for k in (1, 2, 3)
-    ]
-    ring = jnp.stack([ring[k] for k in (0, 3, 2, 1, 0, 3, 2, 1)])
-    column = lax.dynamic_slice_in_dim(ring, (4 - (y >> 1)) & 3, 4, axis=0)
+    column = lax.all_gather(
+        pair.reshape(2 * cols, 2 * rows), "island", axis=0, tiled=True, axis_index_groups=PAIRS
+    )
     weights = lax.all_gather(
-        column.reshape(NY * cols, 2 * rows), "island", axis=0, tiled=True, axis_index_groups=ALONG_X
+        column, "island", axis=0, tiled=True, axis_index_groups=ALONG_X
     )
 
     sent = swap(parts(other, routed, weights))

time: 164 us -> 160 us (0.976)
  blocking collectives: 91.6 us -> 107 us
  starting transfers between devices: 37.9 us -> 23.3 us
  Pallas kernels: 12.4 us -> 8.9 us
    all_gather x1 -> x2, blocking collectives: 15.4 us -> 31.2 us  [the longest x1 15.8 us: local(): lax.all_gather(pair.reshape(2 * cols, 2 * rows), 'island', axis=0, tiled=...]
    ppermute x3 -> x0, starting transfers between devices: 14.8 us -> none  [local(): lax.ppermute(pair, 'island', [(i, (i + 2 * NX * k) % (NX * NY)) for i in...]
    pallas_call x6, Pallas kernels: 8.4 us -> 4.94 us  [the longest x2 2.36 us: parts(): pl.pallas_call(parts_kernel, in_specs=[pl.BlockSpec(memory_space=pltpu.SM...]
    ppermute x3 -> x0, waiting for transfers between devices: 2.89 us -> none  [local(): lax.ppermute(pair, 'island', [(i, (i + 2 * NX * k) % (NX * NY)) for i in...]
  transfers between devices with their start and end apart: 9 -> 6, of which waited for: 6 -> 5; matrix products, arithmetic and copies ran while one was open for 0% -> 0% of each run, Pallas kernels for 5% -> 4%
where the time goes in v5:
time: 160 us; the launch traced here: 159 us
  blocking collectives  107 us (67%)
  starting transfers between devices  23.3 us (15%)
  waiting for transfers between devices  14.8 us (9%)
  Pallas kernels  8.9 us (6%)
  local copies, waits for them, and re-layouts  2.14 us (1%)
  other arithmetic  1.81 us (1%)
    all_to_all x2, blocking collectives, exchange(): lax.all_to_all(x, 'member', split_axis=0, concat_axis=0, tiled=True, axis...  51.1 us
    all_to_all x1, blocking collectives, local(): lax.all_to_all(moved, 'island', split_axis=0, concat_axis=0, tiled=True)  25.1 us
    all_gather x1, blocking collectives, local(): lax.all_gather(pair.reshape(2 * cols, 2 * rows), 'island', axis=0, tiled=...  15.8 us
    all_gather x1, blocking collectives, local(): lax.all_gather(column, 'island', axis=0, tiled=True, axis_index_groups=AL...  15.4 us
    ppermute x2, starting transfers between devices, to_neighbour(): lax.ppermute(x, 'member', [(m, (m + 2 * (by if m % 2 == 0 else -by)) % ME...  10.2 us
    ppermute x2, waiting for transfers between devices, to_neighbour(): lax.ppermute(x, 'member', [(m, (m + 2 * (by if m % 2 == 0 else -by)) % ME...  8.04 us
    all_to_all x1, starting transfers between devices, exchange(): lax.all_to_all(x, 'member', split_axis=0, concat_axis=0, tiled=True, axis...  7.01 us
    pallas_call x1, Pallas kernels, pick(): pl.pallas_call(pick_kernel, grid_spec=pltpu.PrefetchScalarGridSpec(num_sc...  3.95 us
  transfers between devices with their start and end apart: 6, of which 5 were waited for; matrix products, arithmetic and copies ran while one was open for 0% of the time, Pallas kernels for 4%

profile of v5, /device:TPU:8, one launch (start us, length us, event | category | flops | bytes accessed | tf_op | source)
XLA Modules:
  0.0 159.2 jit_solution(6044455055651209584)
XLA Ops:
  0.6 0.8 bitcast_convert_fusion
  1.4 4.3 %collective-permute-start = (bf16[24,320]{1,0:T(8,128)(2,1)S(1)}, bf16[24,320]{1,0:T(8,128)(2,1)S(1)}, u32[]{:S(2)}, u32[]{:S(2)}) collective-permute-start(bf16[24,320]{1,0:T(8,128)(2,1)S(1)} %bitcast_convert_fusion), channel_id=1, source_target_pairs={{0,2},{1,15},{2,4},{3,1},{4,6},{5,3},{6,8},{7,5},{8,10},{9,7},{10,... | collective-permute-start | bytes 46088 | tf_op jit(solution)/shard_map/ppermute | solution.py:26
  5.7 0.0 copy-start
  5.7 1.4 copy-done
  7.1 0.0 copy-start.5
  7.1 0.7 copy-done.5
  7.7 4.0 %pick.1 = bf16[4,2,640,128]{3,2,1,0:T(8,128)(2,1)} custom-call(s32[1]{0:T(128)} %bitcast.2.q_ref, bf16[144,5120]{1,0:T(8,128)(2,1)S(1)} %bitcast.39, s32[1,128]{1,0:T(1,128)S(1)} %copy-done.5), custom_call_target="tpu_custom_call" | custom-call | tf_op jit(solution)/shard_map/pick/pallas_call | solution.py:60
  11.7 2.4 %collective-permute-done = bf16[24,320]{1,0:T(8,128)(2,1)S(1)} collective-permute-done((bf16[24,320]{1,0:T(8,128)(2,1)S(1)}, bf16[24,320]{1,0:T(8,128)(2,1)S(1)}, u32[]{:S(2)}, u32[]{:S(2)}) %collective-permute-start) | collective-permute-done | bytes 15392 | tf_op jit(solution)/shard_map/ppermute | solution.py:26
  14.1 0.1 pad_maximum_fusion
  14.1 7.0 %all-to-all-start = ((bf16[8,640,128]{2,1,0:T(8,128)(2,1)}), bf16[8,640,128]{2,1,0:T(8,128)(2,1)S(1)}, u32[]{:S(2)}, u32[]{:S(2)}) async-start(bf16[8,640,128]{2,1,0:T(8,128)(2,1)} %bitcast.4), calls=%async_computation | async-start | bytes 2621440 | tf_op jit(solution)/shard_map/all_to_all | solution.py:32
  21.2 2.3 %collective-permute-start.1 = (bf16[24,640]{1,0:T(8,128)(2,1)S(1)}, bf16[24,640]{1,0:T(8,128)(2,1)S(1)}, u32[]{:S(2)}, u32[]{:S(2)}) collective-permute-start(bf16[24,640]{1,0:T(8,128)(2,1)S(1)} %pad_maximum_fusion), channel_id=1, source_target_pairs={{0,64},{16,80},{32,96},{48,112},{64,0},{80,16},{96,32},{112,48},{1... | collective-permute-start | bytes 92168 | tf_op jit(solution)/shard_map/ppermute | solution.py:233
  23.5 3.4 %collective-permute-done.1 = bf16[24,640]{1,0:T(8,128)(2,1)S(1)} collective-permute-done((bf16[24,640]{1,0:T(8,128)(2,1)S(1)}, bf16[24,640]{1,0:T(8,128)(2,1)S(1)}, u32[]{:S(2)}, u32[]{:S(2)}) %collective-permute-start.1) | collective-permute-done | bytes 30752 | tf_op jit(solution)/shard_map/ppermute | solution.py:233
  27.0 15.8 %all_gather.6 = bf16[192,640]{1,0:T(8,128)(2,1)S(1)} all-gather(bf16[48,640]{1,0:T(8,128)(2,1)S(1)} %bitcast.44), channel_id=1, replica_groups={{0,128,256,384},{16,144,272,400},{32,160,288,416},{48,176,304,432},{64,..., dimensions={0}, use_global_device_ids=true | all-gather | bytes 307200 | tf_op jit(solution)/shard_map/all_gather | solution.py:238
  42.8 15.4 %all_gather.7.w_ref = bf16[768,640]{1,0:T(8,128)(2,1)S(1)} all-gather(bf16[192,640]{1,0:T(8,128)(2,1)S(1)} %all_gather.6), channel_id=1, replica_groups={{0,16,32,48},{64,80,96,112},{128,144,160,176},{192,208,224,240},{256,27..., dimensions={0}, use_global_device_ids=true | all-gather | bytes 1228800 | tf_op jit(solution)/shard_map/all_gather | solution.py:241
  58.1 0.0 all-to-all-done
  58.1 1.2 parts.3
  59.3 1.9 %collective-permute-start.2 = (bf16[4,768,128]{2,1,0:T(8,128)(2,1)S(1)}, bf16[4,768,128]{2,1,0:T(8,128)(2,1)S(1)}, u32[]{:S(2)}, u32[]{:S(2)}) collective-permute-start(bf16[4,768,128]{2,1,0:T(8,128)(2,1)S(1)} %parts.3), channel_id=1, source_target_pairs={{0,1},{1,0},{2,3},{3,2},{4,5},{5,4},{6,7},{7,6},{8,9},{9,8},{10,11... | collective-permute-start | bytes 2359304 | tf_op jit(solution)/shard_map/ppermute | solution.py:22
  61.2 1.2 parts.2
  62.4 0.0 copy-start.4
  62.4 1.1 collective-permute-done.2
  63.5 0.2 add_convert_fusion
  63.7 28.6 %all_to_all.20.refs_0_ = bf16[4,768,128]{2,1,0:T(8,128)(2,1)S(1)} all-to-all(bf16[4,768,128]{2,1,0:T(8,128)(2,1)S(1)} %add_convert_fusion), channel_id=1, replica_groups={{0,4,8,12},{1,5,9,13},{2,6,10,14},{3,7,11,15},{16,20,24,28},{17,21,25,2..., dimensions={0} | all-to-all | bytes 1572864 | tf_op jit(solution)/shard_map/all_to_all | solution.py:32
  92.3 0.0 copy-done.4
  92.3 0.3 hidden.1
  92.6 22.6 %all_to_all.21.refs_2_ = bf16[4,128,768]{2,1,0:T(8,128)(2,1)S(1)} all-to-all(bf16[4,128,768]{2,1,0:T(8,128)(2,1)S(1)} %hidden.1), channel_id=1, replica_groups={{0,4,8,12},{1,5,9,13},{2,6,10,14},{3,7,11,15},{16,20,24,28},{17,21,25,2..., dimensions={0} | all-to-all | bytes 1572864 | tf_op jit(solution)/shard_map/all_to_all | solution.py:32
  115.1 1.9 %collective-permute-start.3 = (bf16[4,128,768]{2,1,0:T(8,128)(2,1)S(1)}, bf16[4,128,768]{2,1,0:T(8,128)(2,1)S(1)}, u32[]{:S(2)}, u32[]{:S(2)}) collective-permute-start(bf16[4,128,768]{2,1,0:T(8,128)(2,1)S(1)} %all_to_all.21.refs_2_), channel_id=1, source_target_pairs={{0,1},{1,0},{2,3},{3,2},{4,5},{5,4},{6,7},{7,6},{8,9},{9,8},{10,11... | collective-permute-start | bytes 2359304 | tf_op jit(solution)/shard_map/ppermute | solution.py:22
  117.0 2.3 %collective-permute-done.3.refs_3_ = bf16[4,128,768]{2,1,0:T(8,128)(2,1)S(1)} collective-permute-done((bf16[4,128,768]{2,1,0:T(8,128)(2,1)S(1)}, bf16[4,128,768]{2,1,0:T(8,128)(2,1)S(1)}, u32[]{:S(2)}, u32[]{:S(2)}) %collective-permute-start.3) | collective-permute-done | bytes 786464 | tf_op jit(solution)/shard_map/ppermute | solution.py:22
  119.3 0.7 team_grad.3
  120.0 0.0 copy-start.1
  120.0 0.0 copy-start.2
  120.0 0.0 copy-start.3
  120.0 5.9 %collective-permute-start.4 = (bf16[320,768]{1,0:T(8,128)(2,1)S(1)}, bf16[320,768]{1,0:T(8,128)(2,1)S(1)}, u32[]{:S(2)}, u32[]{:S(2)}) collective-permute-start(bf16[320,768]{1,0:T(8,128)(2,1)S(1)} %team_grad.3), channel_id=1, source_target_pairs={{0,14},{1,3},{2,0},{3,5},{4,2},{5,7},{6,4},{7,9},{8,6},{9,11},{10,... | collective-permute-start | bytes 1474568 | tf_op jit(solution)/shard_map/ppermute | solution.py:26
  125.9 0.7 team_grad.2.refs_0_
  126.6 5.6 %collective-permute-done.4.refs_1_ = bf16[320,768]{1,0:T(8,128)(2,1)S(1)} collective-permute-done((bf16[320,768]{1,0:T(8,128)(2,1)S(1)}, bf16[320,768]{1,0:T(8,128)(2,1)S(1)}, u32[]{:S(2)}, u32[]{:S(2)}) %collective-permute-start.4) | collective-permute-done | bytes 491552 | tf_op jit(solution)/shard_map/ppermute | solution.py:26
  132.2 0.0 copy-done.1
  132.3 0.0 copy-done.2
  132.3 0.0 copy-done.3
  132.3 1.0 inner_step.1
  133.2 0.0 copy-start.6
  133.2 0.0 copy-start.7
  133.2 25.1 %all_to_all.22 = bf16[32,64,128]{2,1,0:T(8,128)(2,1)S(1)} all-to-all(bf16[32,64,128]{2,1,0:T(8,128)(2,1)S(1)} %inner_step.1), channel_id=1, replica_groups=mesh['island'=32,'member'=16] {'island'}, dimensions={0} | all-to-all | bytes 1048576 | tf_op jit(solution)/shard_map/all_to_all | solution.py:256
  158.4 0.1 convert_reduce_fusion
  158.5 0.1 fusion.4
  158.5 0.0 copy-done.6
  158.5 0.0 copy-done.7
  158.5 0.6 fusion.2
  (2 shorter events, 0.0 us)
Async XLA Ops:
  1.4 12.7 %collective-permute-start = (bf16[24,320]{1,0:T(8,128)(2,1)S(1)}, bf16[24,320]{1,0:T(8,128)(2,1)S(1)}, u32[]{:S(2)}, u32[]{:S(2)}) collective-permute-start(bf16[24,320]{1,0:T(8,128)(2,1)S(1)} %bitcast_convert_fusion), channel_id=1, source_target_pairs={{0,2},{1,15},{2,4},{3,1},{4,6},{5,3},{6,8},{7,5},{8,10},{9,7},{10,... | collective-permute-start | bytes 46088 | tf_op jit(solution)/shard_map/ppermute | solution.py:26
  5.7 1.4 copy-start
  7.1 0.7 copy-start.5
  14.1 44.0 %all-to-all-start = ((bf16[8,640,128]{2,1,0:T(8,128)(2,1)}), bf16[8,640,128]{2,1,0:T(8,128)(2,1)S(1)}, u32[]{:S(2)}, u32[]{:S(2)}) async-start(bf16[8,640,128]{2,1,0:T(8,128)(2,1)} %bitcast.4), calls=%async_computation | async-start | bytes 2621440 | tf_op jit(solution)/shard_map/all_to_all | solution.py:32
  21.2 5.8 %collective-permute-start.1 = (bf16[24,640]{1,0:T(8,128)(2,1)S(1)}, bf16[24,640]{1,0:T(8,128)(2,1)S(1)}, u32[]{:S(2)}, u32[]{:S(2)}) collective-permute-start(bf16[24,640]{1,0:T(8,128)(2,1)S(1)} %pad_maximum_fusion), channel_id=1, source_target_pairs={{0,64},{16,80},{32,96},{48,112},{64,0},{80,16},{96,32},{112,48},{1... | collective-permute-start | bytes 92168 | tf_op jit(solution)/shard_map/ppermute | solution.py:233
  59.3 4.2 %collective-permute-start.2 = (bf16[4,768,128]{2,1,0:T(8,128)(2,1)S(1)}, bf16[4,768,128]{2,1,0:T(8,128)(2,1)S(1)}, u32[]{:S(2)}, u32[]{:S(2)}) collective-permute-start(bf16[4,768,128]{2,1,0:T(8,128)(2,1)S(1)} %parts.3), channel_id=1, source_target_pairs={{0,1},{1,0},{2,3},{3,2},{4,5},{5,4},{6,7},{7,6},{8,9},{9,8},{10,11... | collective-permute-start | bytes 2359304 | tf_op jit(solution)/shard_map/ppermute | solution.py:22
  62.4 29.9 %copy-start.4 = (bf16[1,128,768]{2,1,0:T(8,128)(2,1)S(1)}, bf16[1,128,768]{2,1,0:T(8,128)(2,1)}, u32[]{:S(2)}) copy-start(bf16[1,128,768]{2,1,0:T(8,128)(2,1)} %param.9) | copy-start | bytes 589828
  115.1 4.2 %collective-permute-start.3 = (bf16[4,128,768]{2,1,0:T(8,128)(2,1)S(1)}, bf16[4,128,768]{2,1,0:T(8,128)(2,1)S(1)}, u32[]{:S(2)}, u32[]{:S(2)}) collective-permute-start(bf16[4,128,768]{2,1,0:T(8,128)(2,1)S(1)} %all_to_all.21.refs_2_), channel_id=1, source_target_pairs={{0,1},{1,0},{2,3},{3,2},{4,5},{5,4},{6,7},{7,6},{8,9},{9,8},{10,11... | collective-permute-start | bytes 2359304 | tf_op jit(solution)/shard_map/ppermute | solution.py:22
  120.0 12.3 %copy-start.1 = (f32[1,320,768]{2,1,0:T(8,128)S(1)}, f32[1,320,768]{2,1,0:T(8,128)}, u32[]{:S(2)}) copy-start(f32[1,320,768]{2,1,0:T(8,128)} %param.13) | copy-start | bytes 2949124
  120.0 12.3 %copy-start.2 = (f32[1,320,768]{2,1,0:T(8,128)S(1)}, f32[1,320,768]{2,1,0:T(8,128)}, u32[]{:S(2)}) copy-start(f32[1,320,768]{2,1,0:T(8,128)} %param.14) | copy-start | bytes 2949124
  120.0 12.2 %copy-start.3 = (bf16[1,320,768]{2,1,0:T(8,128)(2,1)S(1)}, bf16[1,320,768]{2,1,0:T(8,128)(2,1)}, u32[]{:S(2)}) copy-start(bf16[1,320,768]{2,1,0:T(8,128)(2,1)} %param.15) | copy-start | bytes 1474564
  120.0 12.2 %collective-permute-start.4 = (bf16[320,768]{1,0:T(8,128)(2,1)S(1)}, bf16[320,768]{1,0:T(8,128)(2,1)S(1)}, u32[]{:S(2)}, u32[]{:S(2)}) collective-permute-start(bf16[320,768]{1,0:T(8,128)(2,1)S(1)} %team_grad.3), channel_id=1, source_target_pairs={{0,14},{1,3},{2,0},{3,5},{4,2},{5,7},{6,4},{7,9},{8,6},{9,11},{10,... | collective-permute-start | bytes 1474568 | tf_op jit(solution)/shard_map/ppermute | solution.py:26
  133.2 25.3 %copy-start.6 = (f32[320,24]{0,1:T(8,128)S(1)}, f32[320,24]{0,1:T(8,128)}, u32[]{:S(2)}) copy-start(f32[320,24]{0,1:T(8,128)} %param.11) | copy-start | bytes 92164
  133.2 25.3 %copy-start.7 = (f32[320,24]{0,1:T(8,128)S(1)}, f32[320,24]{0,1:T(8,128)}, u32[]{:S(2)}) copy-start(f32[320,24]{0,1:T(8,128)} %param.12) | copy-start | bytes 92164

commit v6 on v5

--- a/solution.py
+++ b/solution.py
@@ -15,6 +15,7 @@
 F32 = jnp.float32
 VMEM = 16 * 2**20
 PACKED = 64
+PIECES = 2
 WHOLE = pl.BlockSpec(memory_space=pltpu.VMEM)
 
 
@@ -34,45 +35,45 @@
     )
 
 
-def pick_kernel(q_ref, tok_ref, slot_ref, out_ref):
-    step = pl.program_id(0)
-    shape = (tok_ref.shape[0], slot_ref.shape[1])
-    chosen = (lax.broadcasted_iota(jnp.int32, shape, 0) == slot_ref[...]).astype(BF)
-    got = lax.dot_general(
-        tok_ref[...], chosen, (((0,), (0,)), ((), ())), preferred_element_type=F32
-    ).astype(BF)
-    rows = got.shape[0] // 2
-    chip = 2 * (step & 3) + ((step >> 2) ^ q_ref[0])
-
-    @pl.when(step < NA)
-    def _():
-        for c in range(2):
-            out_ref[step, c, 0:rows] = got[c * rows : (c + 1) * rows]
-
-    @pl.when(step >= NA)
-    def _():
-        out_ref[((chip + 1) >> 1) & 3, 0, rows : 2 * rows] = got[:rows]
-        out_ref[((chip + 7) >> 1) & 3, 1, rows : 2 * rows] = got[rows:]
+def pick_kernel(q_ref, tok_ref, slot_ref, out_ref, held, slots, sems):
+    parts, tokens, wide = held.shape
+    rows = out_ref.shape[2] // 2
+    fetched = [pltpu.make_async_copy(slot_ref, slots, sems.at[parts])]
+    for p in range(parts):
+        source = tok_ref.at[:, p * wide : (p + 1) * wide]
+        fetched.append(pltpu.make_async_copy(source, held.at[p], sems.at[p]))
+    for copy in fetched:
+        copy.start()
+    fetched[0].wait()
+    chosen = (lax.broadcasted_iota(jnp.int32, (tokens, slots.shape[1]), 0) == slots[...]).astype(BF)
+    for p in range(parts):
+        fetched[p + 1].wait()
+        got = lax.dot_general(
+            held[p], chosen, (((0,), (0,)), ((), ())), preferred_element_type=F32
+        ).astype(BF)
+        for k in range(0, wide, 2 * rows):
+            w = (p * wide + k) // (2 * rows)
+            own = q_ref[0] == w % 2
+            at = pl.ds(pl.multiple_of(jnp.where(own, 0, rows), rows), rows)
+            below = jnp.where(own, w // 2, (w + 1) // 2 % NA)
+            above = jnp.where(own, w // 2, (w + 7) // 2 % NA)
+            out_ref[below, 0, at] = got[k : k + rows]
+            out_ref[above, 1, at] = got[k + rows : k + 2 * rows]
 
 
 def pick(q, tokens, slot_token, rows):
     slots = slot_token.shape[1]
     return pl.pallas_call(
         pick_kernel,
-        grid_spec=pltpu.PrefetchScalarGridSpec(
-            num_scalar_prefetch=1,
-            grid=(2 * NA,),
-            in_specs=[
-                pl.BlockSpec(
-                    (tokens.shape[0], 2 * rows),
-                    lambda i, q: (0, 2 * (i & 3) + ((i >> 2) ^ q[0])),
-                ),
-                pl.BlockSpec((1, slots), lambda i, q: (0, 0)),
-            ],
-            out_specs=pl.BlockSpec((NA, 2, 2 * rows, slots), lambda i, q: (0, 0, 0, 0)),
-        ),
+        in_specs=[pl.BlockSpec(memory_space=pltpu.SMEM)] + [pl.BlockSpec(memory_space=pl.ANY)] * 2,
+        out_specs=WHOLE,
         out_shape=jax.ShapeDtypeStruct((NA, 2, 2 * rows, slots), BF),
-        compiler_params=pltpu.CompilerParams(vmem_limit_bytes=VMEM),
+        scratch_shapes=[
+            pltpu.VMEM((PIECES, tokens.shape[0], tokens.shape[1] // PIECES), BF),
+            pltpu.VMEM((1, slots), jnp.int32),
+            pltpu.SemaphoreType.DMA((PIECES + 1,)),
+        ],
+        compiler_params=pltpu.CompilerParams(vmem_limit_bytes=60 * 2**20),
         name="pick",
     )(q, tokens, slot_token).reshape(2 * NA, 2 * rows, slots)
 

time: 160 us -> 158 us (0.988)
  starting transfers between devices: 23.3 us -> 19.5 us
  waiting for transfers between devices: 14.8 us -> 17.5 us
  local copies, waits for them, and re-layouts: 2.14 us -> 0.11 us
  blocking collectives: 107 us -> 109 us
    ppermute x2, waiting for transfers between devices: 8.04 us -> 10.8 us  [to_neighbour(): lax.ppermute(x, 'member', [(m, (m + 2 * (by if m % 2 == 0 else -by)) % ME...]
    unnamed x16 -> x12, local copies, waits for them, and re-layouts: 2.06 us -> 0.04 us
    all_to_all x1, starting transfers between devices: 7.01 us -> 5.05 us  [exchange(): lax.all_to_all(x, 'member', split_axis=0, concat_axis=0, tiled=True, axis...]
    ppermute x2, starting transfers between devices: 10.2 us -> 8.24 us  [to_neighbour(): lax.ppermute(x, 'member', [(m, (m + 2 * (by if m % 2 == 0 else -by)) % ME...]
where the time goes in v6:
time: 158 us; the launch traced here: 157 us
  blocking collectives  109 us (69%)
  starting transfers between devices  19.5 us (12%)
  waiting for transfers between devices  17.5 us (11%)
  Pallas kernels  8.92 us (6%)
  other arithmetic  1.81 us (1%)
    all_to_all x2, blocking collectives, exchange(): lax.all_to_all(x, 'member', split_axis=0, concat_axis=0, tiled=True, axis...  52.4 us
    all_to_all x1, blocking collectives, local(): lax.all_to_all(moved, 'island', split_axis=0, concat_axis=0, tiled=True)  25.2 us
    all_gather x1, blocking collectives, local(): lax.all_gather(pair.reshape(2 * cols, 2 * rows), 'island', axis=0, tiled=...  15.8 us
    all_gather x1, blocking collectives, local(): lax.all_gather(column, 'island', axis=0, tiled=True, axis_index_groups=AL...  15.4 us
    ppermute x2, waiting for transfers between devices, to_neighbour(): lax.ppermute(x, 'member', [(m, (m + 2 * (by if m % 2 == 0 else -by)) % ME...  10.8 us
    ppermute x2, starting transfers between devices, to_neighbour(): lax.ppermute(x, 'member', [(m, (m + 2 * (by if m % 2 == 0 else -by)) % ME...  8.24 us
    all_to_all x1, starting transfers between devices, exchange(): lax.all_to_all(x, 'member', split_axis=0, concat_axis=0, tiled=True, axis...  5.05 us
    pallas_call x1, Pallas kernels, pick(): pl.pallas_call(pick_kernel, in_specs=[pl.BlockSpec(memory_space=pltpu.SME...  4.01 us
  transfers between devices with their start and end apart: 6, of which 5 were waited for; matrix products, arithmetic and copies ran while one was open for 0% of the time, Pallas kernels for 4%

profile of v6, /device:TPU:8, one launch (start us, length us, event | category | flops | bytes accessed | tf_op | source)
XLA Modules:
  0.0 157.3 jit_solution(5145855884178031027)
XLA Ops:
  0.6 0.8 bitcast_convert_fusion
  1.4 4.3 %collective-permute-start = (bf16[24,320]{1,0:T(8,128)(2,1)S(1)}, bf16[24,320]{1,0:T(8,128)(2,1)S(1)}, u32[]{:S(2)}, u32[]{:S(2)}) collective-permute-start(bf16[24,320]{1,0:T(8,128)(2,1)S(1)} %bitcast_convert_fusion), channel_id=1, source_target_pairs={{0,2},{1,15},{2,4},{3,1},{4,6},{5,3},{6,8},{7,5},{8,10},{9,7},{10,... | collective-permute-start | bytes 46088 | tf_op jit(solution)/shard_map/ppermute | solution.py:27
  5.7 4.0 %pick.1 = bf16[4,2,640,128]{3,2,1,0:T(8,128)(2,1)} custom-call(s32[1]{0:T(128)} %bitcast.2.q_ref, bf16[144,5120]{1,0:T(8,128)(2,1)} %bitcast.44, s32[1,128]{1,0:T(1,128)} %slot_ref.1), custom_call_target="tpu_custom_call" | custom-call | tf_op jit(solution)/shard_map/pick/pallas_call | solution.py:66
  9.7 4.4 %collective-permute-done = bf16[24,320]{1,0:T(8,128)(2,1)S(1)} collective-permute-done((bf16[24,320]{1,0:T(8,128)(2,1)S(1)}, bf16[24,320]{1,0:T(8,128)(2,1)S(1)}, u32[]{:S(2)}, u32[]{:S(2)}) %collective-permute-start) | collective-permute-done | bytes 15392 | tf_op jit(solution)/shard_map/ppermute | solution.py:27
  14.1 0.1 pad_maximum_fusion
  14.1 5.0 %all-to-all-start = ((bf16[8,640,128]{2,1,0:T(8,128)(2,1)}), bf16[8,640,128]{2,1,0:T(8,128)(2,1)S(1)}, u32[]{:S(2)}, u32[]{:S(2)}) async-start(bf16[8,640,128]{2,1,0:T(8,128)(2,1)} %bitcast.43), calls=%async_computation | async-start | bytes 2621440 | tf_op jit(solution)/shard_map/all_to_all | solution.py:33
  19.2 2.3 %collective-permute-start.1 = (bf16[24,640]{1,0:T(8,128)(2,1)S(1)}, bf16[24,640]{1,0:T(8,128)(2,1)S(1)}, u32[]{:S(2)}, u32[]{:S(2)}) collective-permute-start(bf16[24,640]{1,0:T(8,128)(2,1)S(1)} %pad_maximum_fusion), channel_id=1, source_target_pairs={{0,64},{16,80},{32,96},{48,112},{64,0},{80,16},{96,32},{112,48},{1... | collective-permute-start | bytes 92168 | tf_op jit(solution)/shard_map/ppermute | solution.py:234
  21.6 3.4 %collective-permute-done.1 = bf16[24,640]{1,0:T(8,128)(2,1)S(1)} collective-permute-done((bf16[24,640]{1,0:T(8,128)(2,1)S(1)}, bf16[24,640]{1,0:T(8,128)(2,1)S(1)}, u32[]{:S(2)}, u32[]{:S(2)}) %collective-permute-start.1) | collective-permute-done | bytes 30752 | tf_op jit(solution)/shard_map/ppermute | solution.py:234
  25.0 15.8 %all_gather.6 = bf16[192,640]{1,0:T(8,128)(2,1)S(1)} all-gather(bf16[48,640]{1,0:T(8,128)(2,1)S(1)} %bitcast.45), channel_id=1, replica_groups={{0,128,256,384},{16,144,272,400},{32,160,288,416},{48,176,304,432},{64,..., dimensions={0}, use_global_device_ids=true | all-gather | bytes 307200 | tf_op jit(solution)/shard_map/all_gather | solution.py:239
  40.8 15.4 %all_gather.7.w_ref = bf16[768,640]{1,0:T(8,128)(2,1)S(1)} all-gather(bf16[192,640]{1,0:T(8,128)(2,1)S(1)} %all_gather.6), channel_id=1, replica_groups={{0,16,32,48},{64,80,96,112},{128,144,160,176},{192,208,224,240},{256,27..., dimensions={0}, use_global_device_ids=true | all-gather | bytes 1228800 | tf_op jit(solution)/shard_map/all_gather | solution.py:242
  56.2 0.0 all-to-all-done
  56.2 1.2 parts.3
  57.4 1.9 %collective-permute-start.2 = (bf16[4,768,128]{2,1,0:T(8,128)(2,1)S(1)}, bf16[4,768,128]{2,1,0:T(8,128)(2,1)S(1)}, u32[]{:S(2)}, u32[]{:S(2)}) collective-permute-start(bf16[4,768,128]{2,1,0:T(8,128)(2,1)S(1)} %parts.3), channel_id=1, source_target_pairs={{0,1},{1,0},{2,3},{3,2},{4,5},{5,4},{6,7},{7,6},{8,9},{9,8},{10,11... | collective-permute-start | bytes 2359304 | tf_op jit(solution)/shard_map/ppermute | solution.py:23
  59.3 1.2 parts.2
  60.5 0.0 copy-start.3
  60.5 1.1 collective-permute-done.2
  61.5 0.2 add_convert_fusion
  61.7 29.6 %all_to_all.20.refs_0_ = bf16[4,768,128]{2,1,0:T(8,128)(2,1)S(1)} all-to-all(bf16[4,768,128]{2,1,0:T(8,128)(2,1)S(1)} %add_convert_fusion), channel_id=1, replica_groups={{0,4,8,12},{1,5,9,13},{2,6,10,14},{3,7,11,15},{16,20,24,28},{17,21,25,2..., dimensions={0} | all-to-all | bytes 1572864 | tf_op jit(solution)/shard_map/all_to_all | solution.py:33
  91.4 0.0 copy-done.3
  91.4 0.3 hidden.1
  91.6 22.7 %all_to_all.21.refs_2_ = bf16[4,128,768]{2,1,0:T(8,128)(2,1)S(1)} all-to-all(bf16[4,128,768]{2,1,0:T(8,128)(2,1)S(1)} %hidden.1), channel_id=1, replica_groups={{0,4,8,12},{1,5,9,13},{2,6,10,14},{3,7,11,15},{16,20,24,28},{17,21,25,2..., dimensions={0} | all-to-all | bytes 1572864 | tf_op jit(solution)/shard_map/all_to_all | solution.py:33
  114.4 1.9 %collective-permute-start.3 = (bf16[4,128,768]{2,1,0:T(8,128)(2,1)S(1)}, bf16[4,128,768]{2,1,0:T(8,128)(2,1)S(1)}, u32[]{:S(2)}, u32[]{:S(2)}) collective-permute-start(bf16[4,128,768]{2,1,0:T(8,128)(2,1)S(1)} %all_to_all.21.refs_2_), channel_id=1, source_target_pairs={{0,1},{1,0},{2,3},{3,2},{4,5},{5,4},{6,7},{7,6},{8,9},{9,8},{10,11... | collective-permute-start | bytes 2359304 | tf_op jit(solution)/shard_map/ppermute | solution.py:23
  116.3 2.3 %collective-permute-done.3.refs_3_ = bf16[4,128,768]{2,1,0:T(8,128)(2,1)S(1)} collective-permute-done((bf16[4,128,768]{2,1,0:T(8,128)(2,1)S(1)}, bf16[4,128,768]{2,1,0:T(8,128)(2,1)S(1)}, u32[]{:S(2)}, u32[]{:S(2)}) %collective-permute-start.3) | collective-permute-done | bytes 786464 | tf_op jit(solution)/shard_map/ppermute | solution.py:23
  118.6 0.7 team_grad.3
  119.2 0.0 copy-start
  119.3 0.0 copy-start.1
  119.3 0.0 copy-start.2
  119.3 4.0 %collective-permute-start.4 = (bf16[320,768]{1,0:T(8,128)(2,1)S(1)}, bf16[320,768]{1,0:T(8,128)(2,1)S(1)}, u32[]{:S(2)}, u32[]{:S(2)}) collective-permute-start(bf16[320,768]{1,0:T(8,128)(2,1)S(1)} %team_grad.3), channel_id=1, source_target_pairs={{0,14},{1,3},{2,0},{3,5},{4,2},{5,7},{6,4},{7,9},{8,6},{9,11},{10,... | collective-permute-start | bytes 1474568 | tf_op jit(solution)/shard_map/ppermute | solution.py:27
  123.3 0.7 team_grad.2.refs_0_
  123.9 6.4 %collective-permute-done.4.refs_1_ = bf16[320,768]{1,0:T(8,128)(2,1)S(1)} collective-permute-done((bf16[320,768]{1,0:T(8,128)(2,1)S(1)}, bf16[320,768]{1,0:T(8,128)(2,1)S(1)}, u32[]{:S(2)}, u32[]{:S(2)}) %collective-permute-start.4) | collective-permute-done | bytes 491552 | tf_op jit(solution)/shard_map/ppermute | solution.py:27
  130.3 0.0 copy-done
  130.3 0.0 copy-done.1
  130.3 0.0 copy-done.2
  130.3 0.9 inner_step.1
  131.3 0.0 copy-start.4
  131.3 0.0 copy-start.5
  131.3 25.2 %all_to_all.22 = bf16[32,64,128]{2,1,0:T(8,128)(2,1)S(1)} all-to-all(bf16[32,64,128]{2,1,0:T(8,128)(2,1)S(1)} %inner_step.1), channel_id=1, replica_groups=mesh['island'=32,'member'=16] {'island'}, dimensions={0} | all-to-all | bytes 1048576 | tf_op jit(solution)/shard_map/all_to_all | solution.py:257
  156.5 0.1 convert_reduce_fusion
  156.6 0.1 fusion.4
  156.7 0.0 copy-done.4
  156.7 0.0 copy-done.5
  156.7 0.6 fusion.2
  (2 shorter events, 0.0 us)
Async XLA Ops:
  1.4 12.7 %collective-permute-start = (bf16[24,320]{1,0:T(8,128)(2,1)S(1)}, bf16[24,320]{1,0:T(8,128)(2,1)S(1)}, u32[]{:S(2)}, u32[]{:S(2)}) collective-permute-start(bf16[24,320]{1,0:T(8,128)(2,1)S(1)} %bitcast_convert_fusion), channel_id=1, source_target_pairs={{0,2},{1,15},{2,4},{3,1},{4,6},{5,3},{6,8},{7,5},{8,10},{9,7},{10,... | collective-permute-start | bytes 46088 | tf_op jit(solution)/shard_map/ppermute | solution.py:27
  14.1 42.0 %all-to-all-start = ((bf16[8,640,128]{2,1,0:T(8,128)(2,1)}), bf16[8,640,128]{2,1,0:T(8,128)(2,1)S(1)}, u32[]{:S(2)}, u32[]{:S(2)}) async-start(bf16[8,640,128]{2,1,0:T(8,128)(2,1)} %bitcast.43), calls=%async_computation | async-start | bytes 2621440 | tf_op jit(solution)/shard_map/all_to_all | solution.py:33
  19.2 5.8 %collective-permute-start.1 = (bf16[24,640]{1,0:T(8,128)(2,1)S(1)}, bf16[24,640]{1,0:T(8,128)(2,1)S(1)}, u32[]{:S(2)}, u32[]{:S(2)}) collective-permute-start(bf16[24,640]{1,0:T(8,128)(2,1)S(1)} %pad_maximum_fusion), channel_id=1, source_target_pairs={{0,64},{16,80},{32,96},{48,112},{64,0},{80,16},{96,32},{112,48},{1... | collective-permute-start | bytes 92168 | tf_op jit(solution)/shard_map/ppermute | solution.py:234
  57.4 4.2 %collective-permute-start.2 = (bf16[4,768,128]{2,1,0:T(8,128)(2,1)S(1)}, bf16[4,768,128]{2,1,0:T(8,128)(2,1)S(1)}, u32[]{:S(2)}, u32[]{:S(2)}) collective-permute-start(bf16[4,768,128]{2,1,0:T(8,128)(2,1)S(1)} %parts.3), channel_id=1, source_target_pairs={{0,1},{1,0},{2,3},{3,2},{4,5},{5,4},{6,7},{7,6},{8,9},{9,8},{10,11... | collective-permute-start | bytes 2359304 | tf_op jit(solution)/shard_map/ppermute | solution.py:23
  60.5 30.9 %copy-start.3 = (bf16[1,128,768]{2,1,0:T(8,128)(2,1)S(1)}, bf16[1,128,768]{2,1,0:T(8,128)(2,1)}, u32[]{:S(2)}) copy-start(bf16[1,128,768]{2,1,0:T(8,128)(2,1)} %param.9) | copy-start | bytes 589828
  114.4 4.2 %collective-permute-start.3 = (bf16[4,128,768]{2,1,0:T(8,128)(2,1)S(1)}, bf16[4,128,768]{2,1,0:T(8,128)(2,1)S(1)}, u32[]{:S(2)}, u32[]{:S(2)}) collective-permute-start(bf16[4,128,768]{2,1,0:T(8,128)(2,1)S(1)} %all_to_all.21.refs_2_), channel_id=1, source_target_pairs={{0,1},{1,0},{2,3},{3,2},{4,5},{5,4},{6,7},{7,6},{8,9},{9,8},{10,11... | collective-permute-start | bytes 2359304 | tf_op jit(solution)/shard_map/ppermute | solution.py:23
  119.2 11.1 %copy-start = (f32[1,320,768]{2,1,0:T(8,128)S(1)}, f32[1,320,768]{2,1,0:T(8,128)}, u32[]{:S(2)}) copy-start(f32[1,320,768]{2,1,0:T(8,128)} %param.13) | copy-start | bytes 2949124
  119.3 11.1 %copy-start.1 = (f32[1,320,768]{2,1,0:T(8,128)S(1)}, f32[1,320,768]{2,1,0:T(8,128)}, u32[]{:S(2)}) copy-start(f32[1,320,768]{2,1,0:T(8,128)} %param.14) | copy-start | bytes 2949124
  119.3 11.1 %copy-start.2 = (bf16[1,320,768]{2,1,0:T(8,128)(2,1)S(1)}, bf16[1,320,768]{2,1,0:T(8,128)(2,1)}, u32[]{:S(2)}) copy-start(bf16[1,320,768]{2,1,0:T(8,128)(2,1)} %param.15) | copy-start | bytes 1474564
  119.3 11.1 %collective-permute-start.4 = (bf16[320,768]{1,0:T(8,128)(2,1)S(1)}, bf16[320,768]{1,0:T(8,128)(2,1)S(1)}, u32[]{:S(2)}, u32[]{:S(2)}) collective-permute-start(bf16[320,768]{1,0:T(8,128)(2,1)S(1)} %team_grad.3), channel_id=1, source_target_pairs={{0,14},{1,3},{2,0},{3,5},{4,2},{5,7},{6,4},{7,9},{8,6},{9,11},{10,... | collective-permute-start | bytes 1474568 | tf_op jit(solution)/shard_map/ppermute | solution.py:27
  131.3 25.4 %copy-start.4 = (f32[320,24]{0,1:T(8,128)S(1)}, f32[320,24]{0,1:T(8,128)}, u32[]{:S(2)}) copy-start(f32[320,24]{0,1:T(8,128)} %param.11) | copy-start | bytes 92164
  131.3 25.4 %copy-start.5 = (f32[320,24]{0,1:T(8,128)S(1)}, f32[320,24]{0,1:T(8,128)}, u32[]{:S(2)}) copy-start(f32[320,24]{0,1:T(8,128)} %param.12) | copy-start | bytes 92164

commit v7 on v6

--- a/solution.py
+++ b/solution.py
@@ -15,7 +15,7 @@
 F32 = jnp.float32
 VMEM = 16 * 2**20
 PACKED = 64
-PIECES = 2
+PIECES = 1
 WHOLE = pl.BlockSpec(memory_space=pltpu.VMEM)
 
 
@@ -228,9 +228,9 @@
 
     picked = pick(q.reshape(1), tokens[0], slot_token, rows)
 
-    low = weight_t.astype(BF)
-    low = jnp.concatenate([low, to_neighbour(low, 1)], axis=1)
-    picked, low = lax.optimization_barrier((picked, low))
+    far_t = to_neighbour(weight_t, 1)
+    picked, far_t = lax.optimization_barrier((picked, far_t))
+    low = jnp.concatenate([weight_t, far_t], axis=1).astype(BF)
     near = lax.ppermute(low, "island", [(i, i ^ NX) for i in range(NX * NY)])
     routed = exchange(picked, TEAM).reshape(NA, 2, 2 * rows, slots)
     y = lax.axis_index("island") >> 2

time: 158 us -> 157 us (level)
  transfers between devices with their start and end apart: 6 -> 6, of which waited for: 5 -> 5; matrix products, arithmetic and copies ran while one was open for 0% -> 0% of each run, Pallas kernels for 4% -> 3%
where the time goes in v7:
time: 157 us
  blocking collectives  109 us (69%)
  starting transfers between devices  19 us (12%)
  waiting for transfers between devices  18.1 us (12%)
  Pallas kernels  8.32 us (5%)
  other arithmetic  1.88 us (1%)
    all_to_all x2, blocking collectives, exchange(): lax.all_to_all(x, 'member', split_axis=0, concat_axis=0, tiled=True, axis...  52.2 us
    all_to_all x1, blocking collectives, local(): lax.all_to_all(moved, 'island', split_axis=0, concat_axis=0, tiled=True)  25.1 us
    all_gather x1, blocking collectives, local(): lax.all_gather(pair.reshape(2 * cols, 2 * rows), 'island', axis=0, tiled=...  15.9 us
    all_gather x1, blocking collectives, local(): lax.all_gather(column, 'island', axis=0, tiled=True, axis_index_groups=AL...  15.3 us
    ppermute x2, waiting for transfers between devices, to_neighbour(): lax.ppermute(x, 'member', [(m, (m + 2 * (by if m % 2 == 0 else -by)) % ME...  11.3 us
    ppermute x2, starting transfers between devices, to_neighbour(): lax.ppermute(x, 'member', [(m, (m + 2 * (by if m % 2 == 0 else -by)) % ME...  8.36 us
    all_to_all x1, starting transfers between devices, exchange(): lax.all_to_all(x, 'member', split_axis=0, concat_axis=0, tiled=True, axis...  4.47 us
    ppermute x2, starting transfers between devices, swap(): return lax.ppermute(x, 'member', [(m, m ^ 1) for m in range(MEMBERS)])  3.83 us
  transfers between devices with their start and end apart: 6, of which 5 were waited for; matrix products, arithmetic and copies ran while one was open for 0% of the time, Pallas kernels for 3%

profile of v7, /device:TPU:8, one launch (start us, length us, event | category | flops | bytes accessed | tf_op | source)
XLA Modules:
  0.0 156.7 jit_solution(4791721419913903309)
XLA Ops:
  0.6 0.8 bitcast_convert_fusion.1
  1.4 4.3 %collective-permute-start = (bf16[24,320]{1,0:T(8,128)(2,1)S(1)}, bf16[24,320]{1,0:T(8,128)(2,1)S(1)}, u32[]{:S(2)}, u32[]{:S(2)}) collective-permute-start(bf16[24,320]{1,0:T(8,128)(2,1)S(1)} %bitcast_convert_fusion.1), channel_id=1, source_target_pairs={{0,2},{1,15},{2,4},{3,1},{4,6},{5,3},{6,8},{7,5},{8,10},{9,7},{10,... | collective-permute-start | bytes 46088 | tf_op jit(solution)/shard_map/ppermute | solution.py:27
  5.7 3.4 %pick.1 = bf16[4,2,640,128]{3,2,1,0:T(8,128)(2,1)} custom-call(s32[1]{0:T(128)} %bitcast.2.q_ref, bf16[144,5120]{1,0:T(8,128)(2,1)} %bitcast.41, s32[1,128]{1,0:T(1,128)} %slot_ref.1), custom_call_target="tpu_custom_call" | custom-call | tf_op jit(solution)/shard_map/pick/pallas_call | solution.py:66
  9.1 0.0 copy-start.4
  9.1 5.0 %collective-permute-done = bf16[24,320]{1,0:T(8,128)(2,1)S(1)} collective-permute-done((bf16[24,320]{1,0:T(8,128)(2,1)S(1)}, bf16[24,320]{1,0:T(8,128)(2,1)S(1)}, u32[]{:S(2)}, u32[]{:S(2)}) %collective-permute-start) | collective-permute-done | bytes 15392 | tf_op jit(solution)/shard_map/ppermute | solution.py:27
  14.1 4.5 %all-to-all-start = ((bf16[8,640,128]{2,1,0:T(8,128)(2,1)}), bf16[8,640,128]{2,1,0:T(8,128)(2,1)S(1)}, u32[]{:S(2)}, u32[]{:S(2)}) async-start(bf16[8,640,128]{2,1,0:T(8,128)(2,1)} %bitcast.40), calls=%async_computation | async-start | bytes 2621440 | tf_op jit(solution)/shard_map/all_to_all | solution.py:33
  18.5 0.0 copy-done.4
  18.6 0.1 pad_maximum_fusion
  18.6 2.3 %collective-permute-start.1 = (bf16[24,640]{1,0:T(8,128)(2,1)S(1)}, bf16[24,640]{1,0:T(8,128)(2,1)S(1)}, u32[]{:S(2)}, u32[]{:S(2)}) collective-permute-start(bf16[24,640]{1,0:T(8,128)(2,1)S(1)} %pad_maximum_fusion), channel_id=1, source_target_pairs={{0,64},{16,80},{32,96},{48,112},{64,0},{80,16},{96,32},{112,48},{1... | collective-permute-start | bytes 92168 | tf_op jit(solution)/shard_map/ppermute | solution.py:234
  21.0 3.4 %collective-permute-done.1 = bf16[24,640]{1,0:T(8,128)(2,1)S(1)} collective-permute-done((bf16[24,640]{1,0:T(8,128)(2,1)S(1)}, bf16[24,640]{1,0:T(8,128)(2,1)S(1)}, u32[]{:S(2)}, u32[]{:S(2)}) %collective-permute-start.1) | collective-permute-done | bytes 30752 | tf_op jit(solution)/shard_map/ppermute | solution.py:234
  24.4 0.1 maximum_select_fusion
  24.5 15.9 %all_gather.6 = bf16[192,640]{1,0:T(8,128)(2,1)S(1)} all-gather(bf16[48,640]{1,0:T(8,128)(2,1)S(1)} %bitcast.42), channel_id=1, replica_groups={{0,128,256,384},{16,144,272,400},{32,160,288,416},{48,176,304,432},{64,..., dimensions={0}, use_global_device_ids=true | all-gather | bytes 307200 | tf_op jit(solution)/shard_map/all_gather | solution.py:239
  40.4 15.3 %all_gather.7.w_ref = bf16[768,640]{1,0:T(8,128)(2,1)S(1)} all-gather(bf16[192,640]{1,0:T(8,128)(2,1)S(1)} %all_gather.6), channel_id=1, replica_groups={{0,16,32,48},{64,80,96,112},{128,144,160,176},{192,208,224,240},{256,27..., dimensions={0}, use_global_device_ids=true | all-gather | bytes 1228800 | tf_op jit(solution)/shard_map/all_gather | solution.py:242
  55.7 0.0 all-to-all-done
  55.7 1.2 parts.3
  56.9 1.9 %collective-permute-start.2 = (bf16[4,768,128]{2,1,0:T(8,128)(2,1)S(1)}, bf16[4,768,128]{2,1,0:T(8,128)(2,1)S(1)}, u32[]{:S(2)}, u32[]{:S(2)}) collective-permute-start(bf16[4,768,128]{2,1,0:T(8,128)(2,1)S(1)} %parts.3), channel_id=1, source_target_pairs={{0,1},{1,0},{2,3},{3,2},{4,5},{5,4},{6,7},{7,6},{8,9},{9,8},{10,11... | collective-permute-start | bytes 2359304 | tf_op jit(solution)/shard_map/ppermute | solution.py:23
  58.8 1.2 parts.2
  60.0 0.0 copy-start.3
  60.0 1.1 collective-permute-done.2
  61.0 0.2 add_convert_fusion
  61.2 29.6 %all_to_all.20.refs_0_ = bf16[4,768,128]{2,1,0:T(8,128)(2,1)S(1)} all-to-all(bf16[4,768,128]{2,1,0:T(8,128)(2,1)S(1)} %add_convert_fusion), channel_id=1, replica_groups={{0,4,8,12},{1,5,9,13},{2,6,10,14},{3,7,11,15},{16,20,24,28},{17,21,25,2..., dimensions={0} | all-to-all | bytes 1572864 | tf_op jit(solution)/shard_map/all_to_all | solution.py:33
  90.9 0.0 copy-done.3
  90.9 0.3 hidden.1
  91.1 22.6 %all_to_all.21.refs_2_ = bf16[4,128,768]{2,1,0:T(8,128)(2,1)S(1)} all-to-all(bf16[4,128,768]{2,1,0:T(8,128)(2,1)S(1)} %hidden.1), channel_id=1, replica_groups={{0,4,8,12},{1,5,9,13},{2,6,10,14},{3,7,11,15},{16,20,24,28},{17,21,25,2..., dimensions={0} | all-to-all | bytes 1572864 | tf_op jit(solution)/shard_map/all_to_all | solution.py:33
  113.7 1.9 %collective-permute-start.3 = (bf16[4,128,768]{2,1,0:T(8,128)(2,1)S(1)}, bf16[4,128,768]{2,1,0:T(8,128)(2,1)S(1)}, u32[]{:S(2)}, u32[]{:S(2)}) collective-permute-start(bf16[4,128,768]{2,1,0:T(8,128)(2,1)S(1)} %all_to_all.21.refs_2_), channel_id=1, source_target_pairs={{0,1},{1,0},{2,3},{3,2},{4,5},{5,4},{6,7},{7,6},{8,9},{9,8},{10,11... | collective-permute-start | bytes 2359304 | tf_op jit(solution)/shard_map/ppermute | solution.py:23
  115.7 2.3 %collective-permute-done.3.refs_3_ = bf16[4,128,768]{2,1,0:T(8,128)(2,1)S(1)} collective-permute-done((bf16[4,128,768]{2,1,0:T(8,128)(2,1)S(1)}, bf16[4,128,768]{2,1,0:T(8,128)(2,1)S(1)}, u32[]{:S(2)}, u32[]{:S(2)}) %collective-permute-start.3) | collective-permute-done | bytes 786464 | tf_op jit(solution)/shard_map/ppermute | solution.py:23
  117.9 0.7 team_grad.3
  118.6 0.0 copy-start
  118.6 0.0 copy-start.1
  118.6 0.0 copy-start.2
  118.6 4.1 %collective-permute-start.4 = (bf16[320,768]{1,0:T(8,128)(2,1)S(1)}, bf16[320,768]{1,0:T(8,128)(2,1)S(1)}, u32[]{:S(2)}, u32[]{:S(2)}) collective-permute-start(bf16[320,768]{1,0:T(8,128)(2,1)S(1)} %team_grad.3), channel_id=1, source_target_pairs={{0,14},{1,3},{2,0},{3,5},{4,2},{5,7},{6,4},{7,9},{8,6},{9,11},{10,... | collective-permute-start | bytes 1474568 | tf_op jit(solution)/shard_map/ppermute | solution.py:27
  122.7 0.7 team_grad.2.refs_0_
  123.4 6.4 %collective-permute-done.4.refs_1_ = bf16[320,768]{1,0:T(8,128)(2,1)S(1)} collective-permute-done((bf16[320,768]{1,0:T(8,128)(2,1)S(1)}, bf16[320,768]{1,0:T(8,128)(2,1)S(1)}, u32[]{:S(2)}, u32[]{:S(2)}) %collective-permute-start.4) | collective-permute-done | bytes 491552 | tf_op jit(solution)/shard_map/ppermute | solution.py:27
  129.8 0.0 copy-done
  129.8 0.0 copy-done.1
  129.8 0.0 copy-done.2
  129.8 0.9 inner_step.1
  130.8 0.0 copy-start.5
  130.8 25.1 %all_to_all.22 = bf16[32,64,128]{2,1,0:T(8,128)(2,1)S(1)} all-to-all(bf16[32,64,128]{2,1,0:T(8,128)(2,1)S(1)} %inner_step.1), channel_id=1, replica_groups=mesh['island'=32,'member'=16] {'island'}, dimensions={0} | all-to-all | bytes 1048576 | tf_op jit(solution)/shard_map/all_to_all | solution.py:257
  155.9 0.1 convert_reduce_fusion
  156.0 0.1 fusion.3
  156.1 0.0 copy-done.5
  156.1 0.6 fusion.1
  (3 shorter events, 0.0 us)
Async XLA Ops:
  1.4 12.7 %collective-permute-start = (bf16[24,320]{1,0:T(8,128)(2,1)S(1)}, bf16[24,320]{1,0:T(8,128)(2,1)S(1)}, u32[]{:S(2)}, u32[]{:S(2)}) collective-permute-start(bf16[24,320]{1,0:T(8,128)(2,1)S(1)} %bitcast_convert_fusion.1), channel_id=1, source_target_pairs={{0,2},{1,15},{2,4},{3,1},{4,6},{5,3},{6,8},{7,5},{8,10},{9,7},{10,... | collective-permute-start | bytes 46088 | tf_op jit(solution)/shard_map/ppermute | solution.py:27
  9.1 9.4 %copy-start.4 = (f32[320,24]{0,1:T(8,128)S(1)}, f32[320,24]{0,1:T(8,128)}, u32[]{:S(2)}) copy-start(f32[320,24]{0,1:T(8,128)} %param.11) | copy-start | bytes 92164
  14.1 41.6 %all-to-all-start = ((bf16[8,640,128]{2,1,0:T(8,128)(2,1)}), bf16[8,640,128]{2,1,0:T(8,128)(2,1)S(1)}, u32[]{:S(2)}, u32[]{:S(2)}) async-start(bf16[8,640,128]{2,1,0:T(8,128)(2,1)} %bitcast.40), calls=%async_computation | async-start | bytes 2621440 | tf_op jit(solution)/shard_map/all_to_all | solution.py:33
  18.6 5.8 %collective-permute-start.1 = (bf16[24,640]{1,0:T(8,128)(2,1)S(1)}, bf16[24,640]{1,0:T(8,128)(2,1)S(1)}, u32[]{:S(2)}, u32[]{:S(2)}) collective-permute-start(bf16[24,640]{1,0:T(8,128)(2,1)S(1)} %pad_maximum_fusion), channel_id=1, source_target_pairs={{0,64},{16,80},{32,96},{48,112},{64,0},{80,16},{96,32},{112,48},{1... | collective-permute-start | bytes 92168 | tf_op jit(solution)/shard_map/ppermute | solution.py:234
  56.9 4.2 %collective-permute-start.2 = (bf16[4,768,128]{2,1,0:T(8,128)(2,1)S(1)}, bf16[4,768,128]{2,1,0:T(8,128)(2,1)S(1)}, u32[]{:S(2)}, u32[]{:S(2)}) collective-permute-start(bf16[4,768,128]{2,1,0:T(8,128)(2,1)S(1)} %parts.3), channel_id=1, source_target_pairs={{0,1},{1,0},{2,3},{3,2},{4,5},{5,4},{6,7},{7,6},{8,9},{9,8},{10,11... | collective-permute-start | bytes 2359304 | tf_op jit(solution)/shard_map/ppermute | solution.py:23
  60.0 30.9 %copy-start.3 = (bf16[1,128,768]{2,1,0:T(8,128)(2,1)S(1)}, bf16[1,128,768]{2,1,0:T(8,128)(2,1)}, u32[]{:S(2)}) copy-start(bf16[1,128,768]{2,1,0:T(8,128)(2,1)} %param.9) | copy-start | bytes 589828
  113.7 4.2 %collective-permute-start.3 = (bf16[4,128,768]{2,1,0:T(8,128)(2,1)S(1)}, bf16[4,128,768]{2,1,0:T(8,128)(2,1)S(1)}, u32[]{:S(2)}, u32[]{:S(2)}) collective-permute-start(bf16[4,128,768]{2,1,0:T(8,128)(2,1)S(1)} %all_to_all.21.refs_2_), channel_id=1, source_target_pairs={{0,1},{1,0},{2,3},{3,2},{4,5},{5,4},{6,7},{7,6},{8,9},{9,8},{10,11... | collective-permute-start | bytes 2359304 | tf_op jit(solution)/shard_map/ppermute | solution.py:23
  118.6 11.2 %copy-start = (f32[1,320,768]{2,1,0:T(8,128)S(1)}, f32[1,320,768]{2,1,0:T(8,128)}, u32[]{:S(2)}) copy-start(f32[1,320,768]{2,1,0:T(8,128)} %param.13) | copy-start | bytes 2949124
  118.6 11.2 %copy-start.1 = (f32[1,320,768]{2,1,0:T(8,128)S(1)}, f32[1,320,768]{2,1,0:T(8,128)}, u32[]{:S(2)}) copy-start(f32[1,320,768]{2,1,0:T(8,128)} %param.14) | copy-start | bytes 2949124
  118.6 11.2 %copy-start.2 = (bf16[1,320,768]{2,1,0:T(8,128)(2,1)S(1)}, bf16[1,320,768]{2,1,0:T(8,128)(2,1)}, u32[]{:S(2)}) copy-start(bf16[1,320,768]{2,1,0:T(8,128)(2,1)} %param.15) | copy-start | bytes 1474564
  118.6 11.2 %collective-permute-start.4 = (bf16[320,768]{1,0:T(8,128)(2,1)S(1)}, bf16[320,768]{1,0:T(8,128)(2,1)S(1)}, u32[]{:S(2)}, u32[]{:S(2)}) collective-permute-start(bf16[320,768]{1,0:T(8,128)(2,1)S(1)} %team_grad.3), channel_id=1, source_target_pairs={{0,14},{1,3},{2,0},{3,5},{4,2},{5,7},{6,4},{7,9},{8,6},{9,11},{10,... | collective-permute-start | bytes 1474568 | tf_op jit(solution)/shard_map/ppermute | solution.py:27
  130.8 25.3 %copy-start.5 = (f32[320,24]{0,1:T(8,128)S(1)}, f32[320,24]{0,1:T(8,128)}, u32[]{:S(2)}) copy-start(f32[320,24]{0,1:T(8,128)} %param.12) | copy-start | bytes 92164
